TPU v7x, 512 devices: a whole 4x4x16 slice. The times are simulated.
512 devices in a mesh: segment: 8 (over y_lo, x), tile: 64 (over y_hi, z, core).
Axes of the slice: x: 4, y: 4 (y_hi: 2, y_lo: 2; y = y_hi * 2 + y_lo), z: 16, core: 2. Of those that a mesh axis runs over, the one named last changes fastest.
Arguments:
- stored_inputs: bfloat16 [8, 1, 64, 8, 16, 768], P('segment', None, 'tile'), may hold values from -6 to 6
- output_grads: bfloat16 [1, 64, 8, 16, 768], P(None, 'tile'), may hold values from -6 to 6
- norm_gain: float32 [8, 768], P('segment'), may hold values from 0.1 to 1.9
- position_bias: float32 [8, 12, 13, 13], P('segment'), may hold values from -3 to 300
- qkv_weight: bfloat16 [8, 768, 2304], P('segment', 'tile'), may hold values from -0.21875 to 0.21875
- out_weight: bfloat16 [8, 768, 768], P('segment', 'tile'), may hold values from -0.21875 to 0.21875
Outputs:
- input_grads: bfloat16 [8, 1, 64, 8, 16, 768], P('segment', None, 'tile')
All inputs are finite; a program needn't handle non-finite values.
Results may differ from a plain program's by a relative error of at most 0.027.
Values may be sent and summed in bfloat16 or wider, within the bound.
A program may use at most 128 MiB of HBM per device.

v0:
```python
import math

import jax
import jax.numpy as jnp
from jax import lax
from jax.sharding import PartitionSpec as P

D = 768
HEADS = 12
HD = 64
RAD = 6
TH = 8
TW = 16
MICRO = 1


EPSILON = 1e-05
NEG_FILL = -1e30


def shifted(value, axis, steps):
    count = lax.axis_size(axis)
    initial, last = (max(0, -steps), min(count, count - steps))
    return lax.ppermute(value, axis, [(source, source + steps) for source in range(initial, last)])


def dot_trans(left, right):
    return lax.dot_general(
        left, right, (((1,), (1,)), ((), ())), preferred_element_type=jnp.float32
    )


def rim_source(offset, length):
    if offset == -1:
        return slice(length - RAD, length)
    if offset == 0:
        return slice(0, length)
    return slice(0, RAD)


def pad_source(offset, length):
    if offset == -1:
        return slice(0, RAD)
    if offset == 0:
        return slice(RAD, RAD + length)
    return slice(RAD + length, length + 2 * RAD)


def window_tables(position_table, tile_row, tile_col, grid_side):
    pad_rows = TH + 2 * RAD
    pad_cols = TW + 2 * RAD
    window_span = 2 * RAD + 1
    row_offset = (
        jnp.arange(pad_rows, dtype=jnp.int32)[None, :]
        - RAD
        - jnp.arange(TH, dtype=jnp.int32)[:, None]
    )
    col_offset = (
        jnp.arange(pad_cols, dtype=jnp.int32)[None, :]
        - RAD
        - jnp.arange(TW, dtype=jnp.int32)[:, None]
    )
    offsets = jnp.arange(window_span, dtype=jnp.int32) - RAD
    row_onehot = (row_offset[:, :, None] == offsets[None, None, :]).astype(jnp.float32)
    col_onehot = (col_offset[:, :, None] == offsets[None, None, :]).astype(jnp.float32)
    half_table = jnp.einsum(
        "huv,bjv->hubj", position_table, col_onehot, precision=lax.Precision.HIGHEST
    )
    bias_full = jnp.einsum(
        "hubj,aiu->habij", half_table, row_onehot, precision=lax.Precision.HIGHEST
    ).reshape(HEADS, TH * TW, pad_rows * pad_cols)
    global_row = tile_row * TH + jnp.arange(pad_rows, dtype=jnp.int32) - RAD
    global_col = tile_col * TW + jnp.arange(pad_cols, dtype=jnp.int32) - RAD
    row_inside = (global_row >= 0) & (global_row < grid_side * TH)
    col_inside = (global_col >= 0) & (global_col < grid_side * TW)
    row_valid = (jnp.abs(row_offset) <= RAD) & row_inside[None, :]
    col_valid = (jnp.abs(col_offset) <= RAD) & col_inside[None, :]
    valid_pairs = (row_valid[:, None, :, None] & col_valid[None, :, None, :]).reshape(
        TH * TW, pad_rows * pad_cols
    )
    return (bias_full, valid_pairs)


def fill_rim(block, grid_side, tile_col):
    pieces = {}
    for row_step in (-1, 0, 1):
        for col_step in (-1, 0, 1):
            if row_step == 0 and col_step == 0:
                continue
            sent = block[:, rim_source(row_step, TH), rim_source(col_step, TW)]
            received = shifted(sent, "tile", -(row_step * grid_side + col_step))
            keep_mask = (tile_col + col_step >= 0) & (tile_col + col_step < grid_side)
            pieces[row_step, col_step] = jnp.where(keep_mask, received, jnp.zeros_like(received))
    pieces[0, 0] = block
    bands = [
        jnp.concatenate([pieces[row_step, col_step] for col_step in (-1, 0, 1)], axis=2)
        for row_step in (-1, 0, 1)
    ]
    return jnp.concatenate(bands, axis=1)


def return_rim(inner_part, rim_grad, grid_side, tile_col):
    summed = inner_part
    for row_step in (-1, 0, 1):
        for col_step in (-1, 0, 1):
            if row_step == 0 and col_step == 0:
                continue
            sent = rim_grad[pad_source(row_step, TH), pad_source(col_step, TW)]
            received = shifted(sent, "tile", row_step * grid_side + col_step)
            keep_mask = (tile_col - col_step >= 0) & (tile_col - col_step < grid_side)
            addend = jnp.where(keep_mask, received.astype(jnp.float32), 0.0)
            summed = summed.at[rim_source(row_step, TH), rim_source(col_step, TW)].add(addend)
    return summed


def body(stored_inputs, output_grads, norm_gain, position_bias, qkv_weight, out_weight):
    segment_count = lax.axis_size("segment")
    segment_index = lax.axis_index("segment")
    grid_side = math.isqrt(lax.axis_size("tile"))
    tile_index = lax.axis_index("tile")
    tile_row = tile_index // grid_side
    tile_col = tile_index % grid_side
    pad_rows = TH + 2 * RAD
    pad_cols = TW + 2 * RAD
    query_count = TH * TW
    key_count = pad_rows * pad_cols
    stored = stored_inputs[0, :, 0]
    top_grads = output_grads[:, 0]
    gain_row = norm_gain[0]
    qkv_full, out_full = (
        lax.all_gather(qkv_weight[0], "tile", axis=0, tiled=True),
        lax.all_gather(out_weight[0], "tile", axis=0, tiled=True),
    )
    query_weight = qkv_full[:, :D]
    key_weight = qkv_full[:, D : 2 * D]
    value_weight = qkv_full[:, 2 * D :]
    values = stored.astype(jnp.float32)
    center_mean = jnp.mean(values, axis=-1, keepdims=True)
    deviation = values - center_mean
    variance = jnp.mean(deviation * deviation, axis=-1, keepdims=True)
    inverse = lax.rsqrt(variance + EPSILON)
    normal_part = deviation * inverse
    normed = (normal_part * gain_row).astype(jnp.bfloat16)
    flat_normed = normed.reshape(-1, D)
    projected = jnp.dot(flat_normed, qkv_full, preferred_element_type=jnp.float32).astype(
        jnp.bfloat16
    )
    projected = projected.reshape(MICRO, TH, TW, 3 * D)
    queries = projected[..., :D].reshape(MICRO, query_count, D)
    keyvals = fill_rim(projected[..., D:], grid_side, tile_col).reshape(MICRO, key_count, 2 * D)
    bias_full, valid_pairs = window_tables(position_bias[0], tile_row, tile_col, grid_side)

    def forward_part(operands):
        query_now, keyval_now = operands
        query_heads = query_now.reshape(query_count, HEADS, HD)
        key_heads = keyval_now[:, :D].reshape(key_count, HEADS, HD)
        value_heads = keyval_now[:, D:].reshape(key_count, HEADS, HD)
        scores = (
            jnp.einsum("nhd,phd->hnp", query_heads, key_heads, preferred_element_type=jnp.float32)
            * 0.125
        )
        scores = jnp.where(valid_pairs[None], scores + bias_full, NEG_FILL)
        top_score = jnp.max(scores, axis=-1, keepdims=True)
        raw_weight = jnp.exp(scores - top_score)
        probability = raw_weight / jnp.sum(raw_weight, axis=-1, keepdims=True)
        attn_out = jnp.einsum(
            "hnp,phd->nhd",
            probability,
            value_heads.astype(jnp.float32),
            precision=lax.Precision.HIGHEST,
        )
        return (probability.astype(jnp.bfloat16), attn_out)

    prob_all, attn_all = lax.map(forward_part, (queries, keyvals))

    def active_part(operands):
        upstream, query_now, keyval_now, prob_now, attn_now = operands
        grad_attn = dot_trans(upstream.reshape(-1, D), out_full).astype(jnp.bfloat16)
        grad_heads = grad_attn.reshape(query_count, HEADS, HD)
        query_heads = query_now.reshape(query_count, HEADS, HD)
        key_heads = keyval_now[:, :D].reshape(key_count, HEADS, HD)
        value_heads = keyval_now[:, D:].reshape(key_count, HEADS, HD)
        prob_grad = jnp.einsum(
            "nhd,phd->hnp", grad_heads, value_heads, preferred_element_type=jnp.float32
        )
        delta_term = jnp.einsum(
            "nhd,nhd->hn", grad_heads.astype(jnp.float32), attn_now, precision=lax.Precision.HIGHEST
        )[:, :, None]
        score_grad = (prob_now.astype(jnp.float32) * (prob_grad - delta_term)).astype(jnp.bfloat16)
        query_grad = (
            jnp.einsum("hnp,phd->nhd", score_grad, key_heads, preferred_element_type=jnp.float32)
            * 0.125
        )
        key_grad = (
            jnp.einsum("hnp,nhd->phd", score_grad, query_heads, preferred_element_type=jnp.float32)
            * 0.125
        )
        value_grad = jnp.einsum(
            "hnp,nhd->phd", prob_now, grad_heads, preferred_element_type=jnp.float32
        )
        query_low = query_grad.reshape(query_count, D).astype(jnp.bfloat16)
        key_low = key_grad.reshape(key_count, D).astype(jnp.bfloat16)
        value_low = value_grad.reshape(key_count, D).astype(jnp.bfloat16)
        own_part = dot_trans(query_low, query_weight)
        spread = dot_trans(key_low, key_weight) + dot_trans(value_low, value_weight)
        spread = spread.reshape(pad_rows, pad_cols, D)
        inner_part = spread[RAD : RAD + TH, RAD : RAD + TW] + own_part.reshape(TH, TW, D)
        return (inner_part, spread.astype(jnp.bfloat16))

    def spare_part(operands):
        return (
            jnp.zeros((TH, TW, D), jnp.float32),
            jnp.zeros((pad_rows, pad_cols, D), jnp.bfloat16),
        )

    def tick(tick_index, carried):
        incoming, results = carried
        slot_index = tick_index - (segment_count - 1 - segment_index)
        active = (slot_index >= 0) & (slot_index < MICRO)
        slot_safe = jnp.clip(slot_index, 0, MICRO - 1)
        from_top = lax.dynamic_index_in_dim(top_grads, slot_safe, 0, keepdims=False)
        upstream = jnp.where(segment_index == segment_count - 1, from_top, incoming)
        query_now = lax.dynamic_index_in_dim(queries, slot_safe, 0, keepdims=False)
        keyval_now = lax.dynamic_index_in_dim(keyvals, slot_safe, 0, keepdims=False)
        prob_now = lax.dynamic_index_in_dim(prob_all, slot_safe, 0, keepdims=False)
        attn_now = lax.dynamic_index_in_dim(attn_all, slot_safe, 0, keepdims=False)
        inner_part, rim_grad = lax.cond(
            active, active_part, spare_part, (upstream, query_now, keyval_now, prob_now, attn_now)
        )
        token_grad = return_rim(inner_part, rim_grad, grid_side, tile_col)
        part_now = lax.dynamic_index_in_dim(normal_part, slot_safe, 0, keepdims=False)
        inverse_now = lax.dynamic_index_in_dim(inverse, slot_safe, 0, keepdims=False)
        scaled = token_grad * gain_row
        first_mean = jnp.mean(scaled, axis=-1, keepdims=True)
        second_mean = jnp.mean(scaled * part_now, axis=-1, keepdims=True)
        branch = inverse_now * (scaled - first_mean - part_now * second_mean)
        outgoing = (upstream.astype(jnp.float32) + branch).astype(jnp.bfloat16)
        current = lax.dynamic_index_in_dim(results, slot_safe, 0, keepdims=False)
        results = lax.dynamic_update_index_in_dim(
            results, jnp.where(active, outgoing, current), slot_safe, 0
        )
        passed = shifted(outgoing, "segment", -1)
        return (passed, results)

    start_state = (
        jnp.zeros((TH, TW, D), jnp.bfloat16),
        jnp.zeros((MICRO, TH, TW, D), jnp.bfloat16),
    )
    final_pass, results = lax.fori_loop(0, MICRO + segment_count - 1, tick, start_state)
    return results[None, :, None]


def solution(mesh):
    return jax.shard_map(
        body,
        mesh=mesh,
        in_specs=(
            P("segment", None, "tile", None, None, None),
            P(None, "tile", None, None, None),
            P("segment", None),
            P("segment", None, None, None),
            P("segment", "tile", None),
            P("segment", "tile", None),
        ),
        out_specs=P("segment", None, "tile", None, None, None),
        check_vma=False,
    )
```

profile of v0, /device:TPU:1, one launch (start us, length us, event | category | flops | bytes accessed | tf_op | source)
XLA Modules:
  0.0 1248.4 jit_solution(4194244651621949440)
XLA Ops:
  26.2 13.1 %reshape.831 = f32[12,128,560]{2,1,0:T(8,128)} reshape(f32[12,8,16,20,28]{4,3,2,1,0:T(8,128)} %copy.49) | data formatting | bytes 6881280 | tf_op jit(solution)/shard_map/reshape | solution.py:71
  47.1 114.2 %all-gather.7.cloned.1.call-done = bf16[1,768,768]{2,0,1:T(2,128)(2,1)} async-done(((bf16[1,12,768]{2,0,1:T(2,128)(2,1)}), bf16[1,768,768]{2,0,1:T(2,128)(2,1)}) %all-gather.7.cloned.1.call-update) | async-done | bytes 1179664 | tf_op jit(solution)/shard_map/all_gather | solution.py:132
  164.2 155.1 %all-gather.5.cloned.1.call-done = bf16[1,768,2304]{2,0,1:T(2,128)(2,1)} async-done(((bf16[1,12,2304]{2,0,1:T(2,128)(2,1)}), bf16[1,768,2304]{2,0,1:T(2,128)(2,1)}) %all-gather.5.cloned.1.call-update) | async-done | bytes 3538960 | tf_op jit(solution)/shard_map/all_gather | solution.py:131
  333.4 8.7 collective-permute-start.11
  346.2 23.0 %collective-permute-start.12 = (bf16[1,8,6,1536]{3,2,1,0:T(8,128)(2,1)S(1)}, bf16[1,8,6,1536]{3,2,1,0:T(8,128)(2,1)S(1)}, u32[]{:S(2)}, u32[]{:S(2)}) collective-permute-start(bf16[1,8,6,1536]{3,2,1,0:T(8,128)(2,1)S(1)} %get-tuple-element.919), channel_id=1, source_target_pairs={{0,1},{1,2},{2,3},{3,4},{4,5},{5,6},{6,7},{7,8},{8,9},{9,10},{10,1... | collective-permute-start | bytes 442376 | tf_op jit(solution)/shard_map/ppermute | solution.py:24
  371.0 11.2 collective-permute-done.14
  388.8 8.0 collective-permute-done.10
  420.4 821.2 %while.31 = (s32[]{:T(128)}, bf16[8,16,768]{2,1,0:T(8,128)(2,1)S(1)}, bf16[1,8,16,768]{3,2,1,0:T(8,128)(2,1)}, pred[]{:T(512)}, bf16[1,8,16,768]{3,2,1,0:T(8,128...) while((s32[]{:T(128)}, ...), condition=%wide.region_10.11_spmd, body=%wide.region_4.10_spmd.sunk | while | flops 2072176128 | bytes 62982592 | solution.py:249
  443.9 14.8 %collective-permute-start.5 = (bf16[6,6,768]{2,1,0:T(8,128)(2,1)S(1)}, bf16[6,6,768]{2,1,0:T(8,128)(2,1)S(1)}, u32[]{:S(2)}, u32[]{:S(2)}) collective-permute-start(bf16[6,6,768]{2,1,0:T(8,128)(2,1)S(1)} %get-tuple-element.1079), channel_id=1, source_target_pairs={{0,7},{1,8},{2,9},{3,10},{4,11},{5,12},{6,13},{7,14},{8,15},{9,16}... | collective-permute-start | bytes 165896 | tf_op jit(solution)/shard_map/while/body/eval_jaxpr/ppermute | solution.py:24
  461.3 9.5 collective-permute-start.6
  524.6 22.0 %collective-permute-start.5 = (bf16[6,6,768]{2,1,0:T(8,128)(2,1)S(1)}, bf16[6,6,768]{2,1,0:T(8,128)(2,1)S(1)}, u32[]{:S(2)}, u32[]{:S(2)}) collective-permute-start(bf16[6,6,768]{2,1,0:T(8,128)(2,1)S(1)} %get-tuple-element.1079), channel_id=1, source_target_pairs={{0,7},{1,8},{2,9},{3,10},{4,11},{5,12},{6,13},{7,14},{8,15},{9,16}... | collective-permute-start | bytes 165896 | tf_op jit(solution)/shard_map/while/body/eval_jaxpr/ppermute | solution.py:24
  592.9 8.8 collective-permute-start.3
  605.0 9.4 collective-permute-start.5
  680.3 10.1 collective-permute-start.5
  698.4 12.7 %collective-permute-start.6 = (bf16[6,16,768]{2,1,0:T(8,128)(2,1)S(1)}, bf16[6,16,768]{2,1,0:T(8,128)(2,1)S(1)}, u32[]{:S(2)}, u32[]{:S(2)}) collective-permute-start(bf16[6,16,768]{2,1,0:T(8,128)(2,1)S(1)} %get-tuple-element.1082), channel_id=1, source_target_pairs={{0,8},{1,9},{2,10},{3,11},{4,12},{5,13},{6,14},{7,15},{8,16},{9,17... | collective-permute-start | bytes 442376 | tf_op jit(solution)/shard_map/while/body/eval_jaxpr/ppermute | solution.py:24
  763.7 11.4 collective-permute-start.5
  777.7 9.7 collective-permute-start.6
  810.4 14.5 %collective-permute-done.8 = bf16[8,16,768]{2,1,0:T(8,128)(2,1)S(1)} collective-permute-done((bf16[8,16,768]{2,1,0:T(8,128)(2,1)S(1)}, bf16[8,16,768]{2,1,0:T(8,128)(2,1)S(1)}, u32[]{:S(2)}, u32[]{:S(2)}) %collective-permute-start.8) | collective-permute-done | bytes 196640 | tf_op jit(solution)/shard_map/while/body/eval_jaxpr/ppermute | solution.py:24
  845.5 10.5 collective-permute-start.5
  858.5 8.1 collective-permute-start.6
  965.2 172.0 %collective-permute-done.8 = bf16[8,16,768]{2,1,0:T(8,128)(2,1)S(1)} collective-permute-done((bf16[8,16,768]{2,1,0:T(8,128)(2,1)S(1)}, bf16[8,16,768]{2,1,0:T(8,128)(2,1)S(1)}, u32[]{:S(2)}, u32[]{:S(2)}) %collective-permute-start.8) | collective-permute-done | bytes 196640 | tf_op jit(solution)/shard_map/while/body/eval_jaxpr/ppermute | solution.py:24
  1138.2 27.1 %conditional.2 = (f32[8,16,768]{2,1,0:T(8,128)}, bf16[20,28,768]{2,1,0:T(8,128)(2,1)}, f32[6,6,768]{2,1,0:T(8,128)}) conditional(s32[]{:T(128)} %convert_element_type.258, () %tuple.161, (bf16[1,12,128,560]{2,3,1,0:T(8,128)(2,1)}, bf16[8,16,768]{2,1,0:T(8,128)(2,1)S(1)}, bf16[768,768]{1,0:T(8,128)(2,1)}, bf16[1,560,1536]{1,2,0:T(8,128)(2,1)}, ...), branch_computations={%region_5.5_spmd, %region_6.6_spmd} | conditional | flops 2069776896 | bytes 48291948 | solution.py:227
  1179.5 11.1 collective-permute-done
  1205.8 10.6 collective-permute-start.7
  (501 shorter events, 582.1 us)
Async XLA Ops:
  6.5 154.8 %all-gather.7.cloned.1.call-start = ((), (), s32[]{:S(2)}) async-start(), calls=%async_computation.1 | async-start | bytes 2396160 | tf_op jit(solution)/shard_map/all_gather | solution.py:132
  7.9 311.3 %all-gather.5.cloned.1.call-start = ((), (), s32[]{:S(2)}) async-start(), calls=%async_computation | async-start | bytes 7188480 | tf_op jit(solution)/shard_map/all_gather | solution.py:131
  327.5 61.2 %collective-permute-start.15 = (bf16[1,6,16,1536]{3,2,1,0:T(8,128)(2,1)S(1)}, bf16[1,6,16,1536]{3,2,1,0:T(8,128)(2,1)S(1)}, u32[]{:S(2)}, u32[]{:S(2)}) collective-permute-start(bf16[1,6,16,1536]{3,2,1,0:T(8,128)(2,1)S(1)} %get-tuple-element.918), channel_id=1, source_target_pairs={{8,0},{9,1},{10,2},{11,3},{12,4},{13,5},{14,6},{15,7},{16,8},{17,9... | collective-permute-start | bytes 884744 | tf_op jit(solution)/shard_map/ppermute | solution.py:24
  328.8 53.4 %collective-permute-start.14 = (bf16[1,6,6,1536]{3,2,1,0:T(8,128)(2,1)S(1)}, bf16[1,6,6,1536]{3,2,1,0:T(8,128)(2,1)}, u32[]{:S(2)}, u32[]{:S(2)}) collective-permute-start(bf16[1,6,6,1536]{3,2,1,0:T(8,128)(2,1)S(1)} %get-tuple-element.915), channel_id=1, source_target_pairs={{7,0},{8,1},{9,2},{10,3},{11,4},{12,5},{13,6},{14,7},{15,8},{16,9}... | collective-permute-start | bytes 331784 | tf_op jit(solution)/shard_map/ppermute | solution.py:24
  330.1 58.5 %collective-permute-start.13 = (bf16[1,8,6,1536]{3,2,1,0:T(8,128)(2,1)S(1)}, bf16[1,8,6,1536]{3,2,1,0:T(8,128)(2,1)S(1)}, u32[]{:S(2)}, u32[]{:S(2)}) collective-permute-start(bf16[1,8,6,1536]{3,2,1,0:T(8,128)(2,1)S(1)} %get-tuple-element.920), channel_id=1, source_target_pairs={{1,0},{2,1},{3,2},{4,3},{5,4},{6,5},{7,6},{8,7},{9,8},{10,9},{11,1... | collective-permute-start | bytes 442376 | tf_op jit(solution)/shard_map/ppermute | solution.py:24
  346.2 42.5 %collective-permute-start.12 = (bf16[1,8,6,1536]{3,2,1,0:T(8,128)(2,1)S(1)}, bf16[1,8,6,1536]{3,2,1,0:T(8,128)(2,1)S(1)}, u32[]{:S(2)}, u32[]{:S(2)}) collective-permute-start(bf16[1,8,6,1536]{3,2,1,0:T(8,128)(2,1)S(1)} %get-tuple-element.919), channel_id=1, source_target_pairs={{0,1},{1,2},{2,3},{3,4},{4,5},{5,6},{6,7},{7,8},{8,9},{9,10},{10,1... | collective-permute-start | bytes 442376 | tf_op jit(solution)/shard_map/ppermute | solution.py:24
  428.7 43.8 %collective-permute-start.2 = (bf16[6,6,768]{2,1,0:T(8,128)(2,1)S(1)}, bf16[6,6,768]{2,1,0:T(8,128)(2,1)S(1)}, u32[]{:S(2)}, u32[]{:S(2)}) collective-permute-start(bf16[6,6,768]{2,1,0:T(8,128)(2,1)S(1)} %get-tuple-element.1076), channel_id=1, source_target_pairs={{7,0},{8,1},{9,2},{10,3},{11,4},{12,5},{13,6},{14,7},{15,8},{16,9}... | collective-permute-start | bytes 165896 | tf_op jit(solution)/shard_map/while/body/eval_jaxpr/ppermute | solution.py:24
  431.1 50.6 %collective-permute-start.3 = (bf16[8,6,768]{2,1,0:T(8,128)(2,1)S(1)}, bf16[8,6,768]{2,1,0:T(8,128)(2,1)S(1)}, u32[]{:S(2)}, u32[]{:S(2)}) collective-permute-start(bf16[8,6,768]{2,1,0:T(8,128)(2,1)S(1)} %get-tuple-element.1077), channel_id=1, source_target_pairs={{1,0},{2,1},{3,2},{4,3},{5,4},{6,5},{7,6},{8,7},{9,8},{10,9},{11,1... | collective-permute-start | bytes 221192 | tf_op jit(solution)/shard_map/while/body/eval_jaxpr/ppermute | solution.py:24
  436.6 47.7 %collective-permute-start.4 = (bf16[8,6,768]{2,1,0:T(8,128)(2,1)S(1)}, bf16[8,6,768]{2,1,0:T(8,128)(2,1)S(1)}, u32[]{:S(2)}, u32[]{:S(2)}) collective-permute-start(bf16[8,6,768]{2,1,0:T(8,128)(2,1)S(1)} %get-tuple-element.1078), channel_id=1, source_target_pairs={{0,1},{1,2},{2,3},{3,4},{4,5},{5,6},{6,7},{7,8},{8,9},{9,10},{10,1... | collective-permute-start | bytes 221192 | tf_op jit(solution)/shard_map/while/body/eval_jaxpr/ppermute | solution.py:24
  443.9 43.2 %collective-permute-start.5 = (bf16[6,6,768]{2,1,0:T(8,128)(2,1)S(1)}, bf16[6,6,768]{2,1,0:T(8,128)(2,1)S(1)}, u32[]{:S(2)}, u32[]{:S(2)}) collective-permute-start(bf16[6,6,768]{2,1,0:T(8,128)(2,1)S(1)} %get-tuple-element.1079), channel_id=1, source_target_pairs={{0,7},{1,8},{2,9},{3,10},{4,11},{5,12},{6,13},{7,14},{8,15},{9,16}... | collective-permute-start | bytes 165896 | tf_op jit(solution)/shard_map/while/body/eval_jaxpr/ppermute | solution.py:24
  513.5 42.3 %collective-permute-start.2 = (bf16[6,6,768]{2,1,0:T(8,128)(2,1)S(1)}, bf16[6,6,768]{2,1,0:T(8,128)(2,1)S(1)}, u32[]{:S(2)}, u32[]{:S(2)}) collective-permute-start(bf16[6,6,768]{2,1,0:T(8,128)(2,1)S(1)} %get-tuple-element.1076), channel_id=1, source_target_pairs={{7,0},{8,1},{9,2},{10,3},{11,4},{12,5},{13,6},{14,7},{15,8},{16,9}... | collective-permute-start | bytes 165896 | tf_op jit(solution)/shard_map/while/body/eval_jaxpr/ppermute | solution.py:24
  515.8 43.0 %collective-permute-start.3 = (bf16[8,6,768]{2,1,0:T(8,128)(2,1)S(1)}, bf16[8,6,768]{2,1,0:T(8,128)(2,1)S(1)}, u32[]{:S(2)}, u32[]{:S(2)}) collective-permute-start(bf16[8,6,768]{2,1,0:T(8,128)(2,1)S(1)} %get-tuple-element.1077), channel_id=1, source_target_pairs={{1,0},{2,1},{3,2},{4,3},{5,4},{6,5},{7,6},{8,7},{9,8},{10,9},{11,1... | collective-permute-start | bytes 221192 | tf_op jit(solution)/shard_map/while/body/eval_jaxpr/ppermute | solution.py:24
  521.3 40.1 %collective-permute-start.4 = (bf16[8,6,768]{2,1,0:T(8,128)(2,1)S(1)}, bf16[8,6,768]{2,1,0:T(8,128)(2,1)S(1)}, u32[]{:S(2)}, u32[]{:S(2)}) collective-permute-start(bf16[8,6,768]{2,1,0:T(8,128)(2,1)S(1)} %get-tuple-element.1078), channel_id=1, source_target_pairs={{0,1},{1,2},{2,3},{3,4},{4,5},{5,6},{6,7},{7,8},{8,9},{9,10},{10,1... | collective-permute-start | bytes 221192 | tf_op jit(solution)/shard_map/while/body/eval_jaxpr/ppermute | solution.py:24
  590.5 40.0 %collective-permute-start.2 = (bf16[6,6,768]{2,1,0:T(8,128)(2,1)S(1)}, bf16[6,6,768]{2,1,0:T(8,128)(2,1)S(1)}, u32[]{:S(2)}, u32[]{:S(2)}) collective-permute-start(bf16[6,6,768]{2,1,0:T(8,128)(2,1)S(1)} %get-tuple-element.1076), channel_id=1, source_target_pairs={{7,0},{8,1},{9,2},{10,3},{11,4},{12,5},{13,6},{14,7},{15,8},{16,9}... | collective-permute-start | bytes 165896 | tf_op jit(solution)/shard_map/while/body/eval_jaxpr/ppermute | solution.py:24
  592.9 42.7 %collective-permute-start.3 = (bf16[8,6,768]{2,1,0:T(8,128)(2,1)S(1)}, bf16[8,6,768]{2,1,0:T(8,128)(2,1)S(1)}, u32[]{:S(2)}, u32[]{:S(2)}) collective-permute-start(bf16[8,6,768]{2,1,0:T(8,128)(2,1)S(1)} %get-tuple-element.1077), channel_id=1, source_target_pairs={{1,0},{2,1},{3,2},{4,3},{5,4},{6,5},{7,6},{8,7},{9,8},{10,9},{11,1... | collective-permute-start | bytes 221192 | tf_op jit(solution)/shard_map/while/body/eval_jaxpr/ppermute | solution.py:24
  667.3 45.5 %collective-permute-start.2 = (bf16[6,6,768]{2,1,0:T(8,128)(2,1)S(1)}, bf16[6,6,768]{2,1,0:T(8,128)(2,1)S(1)}, u32[]{:S(2)}, u32[]{:S(2)}) collective-permute-start(bf16[6,6,768]{2,1,0:T(8,128)(2,1)S(1)} %get-tuple-element.1076), channel_id=1, source_target_pairs={{7,0},{8,1},{9,2},{10,3},{11,4},{12,5},{13,6},{14,7},{15,8},{16,9}... | collective-permute-start | bytes 165896 | tf_op jit(solution)/shard_map/while/body/eval_jaxpr/ppermute | solution.py:24
  669.7 46.2 %collective-permute-start.3 = (bf16[8,6,768]{2,1,0:T(8,128)(2,1)S(1)}, bf16[8,6,768]{2,1,0:T(8,128)(2,1)S(1)}, u32[]{:S(2)}, u32[]{:S(2)}) collective-permute-start(bf16[8,6,768]{2,1,0:T(8,128)(2,1)S(1)} %get-tuple-element.1077), channel_id=1, source_target_pairs={{1,0},{2,1},{3,2},{4,3},{5,4},{6,5},{7,6},{8,7},{9,8},{10,9},{11,1... | collective-permute-start | bytes 221192 | tf_op jit(solution)/shard_map/while/body/eval_jaxpr/ppermute | solution.py:24
  677.0 41.5 %collective-permute-start.4 = (bf16[8,6,768]{2,1,0:T(8,128)(2,1)S(1)}, bf16[8,6,768]{2,1,0:T(8,128)(2,1)S(1)}, u32[]{:S(2)}, u32[]{:S(2)}) collective-permute-start(bf16[8,6,768]{2,1,0:T(8,128)(2,1)S(1)} %get-tuple-element.1078), channel_id=1, source_target_pairs={{0,1},{1,2},{2,3},{3,4},{4,5},{5,6},{6,7},{7,8},{8,9},{9,10},{10,1... | collective-permute-start | bytes 221192 | tf_op jit(solution)/shard_map/while/body/eval_jaxpr/ppermute | solution.py:24
  680.3 40.9 %collective-permute-start.5 = (bf16[6,6,768]{2,1,0:T(8,128)(2,1)S(1)}, bf16[6,6,768]{2,1,0:T(8,128)(2,1)S(1)}, u32[]{:S(2)}, u32[]{:S(2)}) collective-permute-start(bf16[6,6,768]{2,1,0:T(8,128)(2,1)S(1)} %get-tuple-element.1079), channel_id=1, source_target_pairs={{0,7},{1,8},{2,9},{3,10},{4,11},{5,12},{6,13},{7,14},{8,15},{9,16}... | collective-permute-start | bytes 165896 | tf_op jit(solution)/shard_map/while/body/eval_jaxpr/ppermute | solution.py:24
  748.8 40.4 %collective-permute-start.2 = (bf16[6,6,768]{2,1,0:T(8,128)(2,1)S(1)}, bf16[6,6,768]{2,1,0:T(8,128)(2,1)S(1)}, u32[]{:S(2)}, u32[]{:S(2)}) collective-permute-start(bf16[6,6,768]{2,1,0:T(8,128)(2,1)S(1)} %get-tuple-element.1076), channel_id=1, source_target_pairs={{7,0},{8,1},{9,2},{10,3},{11,4},{12,5},{13,6},{14,7},{15,8},{16,9}... | collective-permute-start | bytes 165896 | tf_op jit(solution)/shard_map/while/body/eval_jaxpr/ppermute | solution.py:24
  751.1 41.1 %collective-permute-start.3 = (bf16[8,6,768]{2,1,0:T(8,128)(2,1)S(1)}, bf16[8,6,768]{2,1,0:T(8,128)(2,1)S(1)}, u32[]{:S(2)}, u32[]{:S(2)}) collective-permute-start(bf16[8,6,768]{2,1,0:T(8,128)(2,1)S(1)} %get-tuple-element.1077), channel_id=1, source_target_pairs={{1,0},{2,1},{3,2},{4,3},{5,4},{6,5},{7,6},{8,7},{9,8},{10,9},{11,1... | collective-permute-start | bytes 221192 | tf_op jit(solution)/shard_map/while/body/eval_jaxpr/ppermute | solution.py:24
  963.9 173.3 %collective-permute-start.8 = (bf16[8,16,768]{2,1,0:T(8,128)(2,1)S(1)}, bf16[8,16,768]{2,1,0:T(8,128)(2,1)S(1)}, u32[]{:S(2)}, u32[]{:S(2)}) collective-permute-start(bf16[8,16,768]{2,1,0:T(8,128)(2,1)S(1)} %get-tuple-element.1090), channel_id=1, source_target_pairs={{64,0},{128,64},{192,128},{256,192},{320,256},{384,320},{448,384},... | collective-permute-start | bytes 589832 | tf_op jit(solution)/shard_map/while/body/eval_jaxpr/ppermute | solution.py:24
  1172.5 45.6 %collective-permute-start.3 = (bf16[8,6,768]{2,1,0:T(8,128)(2,1)S(1)}, bf16[8,6,768]{2,1,0:T(8,128)(2,1)S(1)}, u32[]{:S(2)}, u32[]{:S(2)}) collective-permute-start(bf16[8,6,768]{2,1,0:T(8,128)(2,1)S(1)} %get-tuple-element.1077), channel_id=1, source_target_pairs={{1,0},{2,1},{3,2},{4,3},{5,4},{6,5},{7,6},{8,7},{9,8},{10,9},{11,1... | collective-permute-start | bytes 221192 | tf_op jit(solution)/shard_map/while/body/eval_jaxpr/ppermute | solution.py:24
  1176.1 44.7 %collective-permute-start.4 = (bf16[8,6,768]{2,1,0:T(8,128)(2,1)S(1)}, bf16[8,6,768]{2,1,0:T(8,128)(2,1)S(1)}, u32[]{:S(2)}, u32[]{:S(2)}) collective-permute-start(bf16[8,6,768]{2,1,0:T(8,128)(2,1)S(1)} %get-tuple-element.1078), channel_id=1, source_target_pairs={{0,1},{1,2},{2,3},{3,4},{4,5},{5,6},{6,7},{7,8},{8,9},{9,10},{10,1... | collective-permute-start | bytes 221192 | tf_op jit(solution)/shard_map/while/body/eval_jaxpr/ppermute | solution.py:24
  (83 other events, 1813.6 us)
Sparse Core Ops, SparseCore 0:
  10.6 150.7 all-gather.6
  164.4 154.8 all-gather.4
where the time goes:
time: 1260 us; the launch traced here: 1250 us
  waiting for transfers between devices  551 us (44%)
  starting transfers between devices  332 us (26%)
  local copies, waits for them, and re-layouts  201 us (16%)
  other arithmetic  116 us (9%)
  matrix products  32.5 us (3%)
  between operations  13.9 us (1%)
    ppermute x80, starting transfers between devices, shifted(): lax.ppermute(value, axis, [(source, source + steps) for source in range(i...  332 us
    ppermute x80, waiting for transfers between devices, shifted(): lax.ppermute(value, axis, [(source, source + steps) for source in range(i...  282 us
    all_gather x1, waiting for transfers between devices, body(): lax.all_gather(qkv_weight[0], 'tile', axis=0, tiled=True)  155 us
    all_gather x1, waiting for transfers between devices, body(): lax.all_gather(out_weight[0], 'tile', axis=0, tiled=True)  114 us
    scatter-add x48, local copies, waits for them, and re-layouts, return_rim(): summed.at[rim_source(row_step, TH), rim_source(col_step, TW)].add(addend)  90.6 us
    another operation x32, other arithmetic  29.5 us
    scatter-add x16, other arithmetic, return_rim(): summed.at[rim_source(row_step, TH), rim_source(col_step, TW)].add(addend)  27.5 us
    slice x24, local copies, waits for them, and re-layouts, return_rim(): sent = rim_grad[pad_source(row_step, TH), pad_source(col_step, TW)]  26.2 us
  transfers between devices with their start and end apart: 82, of which 21 were waited for; matrix products, arithmetic and copies ran while one was open for 18% of the time, Pallas kernels for 0%

commit v1 on v0

v1 whole, which is shorter than its diff:
```python
import functools

import jax
import jax.numpy as jnp
from jax import lax
from jax.experimental import pallas as pl
from jax.experimental.pallas import tpu as pltpu
from jax.sharding import PartitionSpec as P

D = 768
HEADS = 12
RAD = 6
TH = 8
TW = 16
PAIRS = HEADS // 2
WIDE = 3 * D
OLW = D + 128
EPSILON = 1e-05
NEG_FILL = -1e30
MESH = pl.DeviceIdType.MESH
BF16 = jnp.bfloat16
F32 = jnp.float32

SLOTS = 640
GROUP = 160
T0, B0 = GROUP, 2 * GROUP
OWN_T, OWN_B = T0 + 48, B0 + 48


class Place:
    def __init__(self, tile_count):
        self.zs = tile_count // 4
        self.cols = self.zs // 2
        self.seg = lax.axis_index("segment")
        self.tile = lax.axis_index("tile")
        self.yh = self.tile // (2 * self.zs)
        self.z = (self.tile % (2 * self.zs)) // 2
        self.core = self.tile % 2
        self.rb = self.yh * 2 + self.core
        self.left = self.at(self.yh, (self.z + self.zs - 1) % self.zs, self.core)
        self.right = self.at(self.yh, (self.z + 1) % self.zs, self.core)
        self.mate = self.at(self.yh, self.z, 1 - self.core)
        self.cross = self.at(1 - self.yh, self.z, self.core)
        self.has_up = self.rb > 0
        self.has_down = self.rb < 3
        up = (self.rb + 3) % 4
        down = (self.rb + 1) % 4
        self.up = self.at(up // 2, self.z, up % 2)
        self.down = self.at(down // 2, self.z, down % 2)
        self.row = self.tile // self.cols
        self.col = self.tile % self.cols
        self.half = self.z % 2
        self.tile_t = (2 * self.rb) * self.cols + self.z // 2
        self.tile_b = (2 * self.rb + 1) * self.cols + self.z // 2

    def at(self, yh, z, core):
        return yh * (2 * self.zs) + z * 2 + core

    def block_of(self, half):
        rb = self.row // 2
        return self.at(rb // 2, 2 * self.col + half, rb % 2)


def remote(src, dst, send, recv, device):
    return pltpu.make_async_remote_copy(
        src_ref=src, dst_ref=dst, send_sem=send, recv_sem=recv, device_id=device, device_id_type=MESH
    )


def signal(sem, device):
    pl.semaphore_signal(sem, inc=1, device_id=device, device_id_type=MESH)


def one(flag):
    return jnp.where(flag, 1, 0).astype(jnp.int32)


def side_copies(place, buf, base, send, recv, at):
    left = (place.seg, place.left)
    right = (place.seg, place.right)
    return [
        remote(
            buf.at[pl.ds(base + 48, 48)], buf.at[pl.ds(base + 112, 48)],
            send.at[at], recv.at[at], left,
        ),
        remote(
            buf.at[pl.ds(base + 64, 48)], buf.at[pl.ds(base, 48)],
            send.at[at + 1], recv.at[at + 1], right,
        ),
    ]


class Vertical:
    def __init__(self, place, buf, send, recv, at):
        self.place = place
        self.go_up = remote(
            buf.at[pl.ds(T0, GROUP)], buf.at[pl.ds(3 * GROUP, GROUP)],
            send.at[at], recv.at[at], (place.seg, place.up),
        )
        self.go_down = remote(
            buf.at[pl.ds(B0, GROUP)], buf.at[pl.ds(0, GROUP)],
            send.at[at + 1], recv.at[at + 1], (place.seg, place.down),
        )

    def start(self):
        pl.when(self.place.has_up)(self.go_up.start)
        pl.when(self.place.has_down)(self.go_down.start)

    def wait_recv(self):
        pl.when(self.place.has_down)(self.go_up.wait_recv)
        pl.when(self.place.has_up)(self.go_down.wait_recv)

    def wait_send(self):
        pl.when(self.place.has_up)(self.go_up.wait_send)
        pl.when(self.place.has_down)(self.go_down.wait_send)


def clear_outside(place, buf):
    blank = jnp.zeros((GROUP, buf.shape[1]), buf.dtype)

    @pl.when(jnp.logical_not(place.has_up))
    def _():
        buf[0:GROUP, :] = blank

    @pl.when(jnp.logical_not(place.has_down))
    def _():
        buf[3 * GROUP : SLOTS, :] = blank


def gather_kernel(
    tile_count, pack_ref, x_ref, g_ref, all_ref, slots_ref, top_ref,
    ring_send, ring_recv, mate_send, mate_recv, send, recv, local,
):
    place = Place(tile_count)
    seg = place.seg
    zs = place.zs
    targets = [place.block_of(0), place.block_of(1)]
    sources = [place.tile_t, place.tile_b]
    barrier = pltpu.get_barrier_semaphore()
    for device in (place.left, place.right, place.mate, place.cross):
        signal(barrier, (seg, device))
    count = jnp.int32(4)

    @pl.when(place.has_up)
    def _():
        signal(barrier, (seg, place.up))

    @pl.when(place.has_down)
    def _():
        signal(barrier, (seg, place.down))

    count = count + one(place.has_up) + one(place.has_down)
    for source in sources:

        @pl.when(source != place.tile)
        def _():
            signal(barrier, (seg, source))

    for target in targets:
        count = count + one(target != place.tile)

    all_ref[place.z, place.core, place.yh] = pack_ref[...]
    clear_outside(place, slots_ref)
    pl.semaphore_wait(barrier, count)

    mine = all_ref.at[place.z, place.core, place.yh]
    theirs = all_ref.at[place.z, place.core, 1 - place.yh]
    over = remote(mine, mine, send.at[12], recv.at[12], (seg, place.cross))
    over.start()

    group = place.row % 2
    x_at = pl.multiple_of(OWN_T + group * GROUP, 16)
    g_at = pl.multiple_of(group * 64, 16)

    def moves(half):
        device = (seg, targets[half])
        rows = pl.ds(half * 64, 64)
        return (
            remote(x_ref.at[rows], slots_ref.at[pl.ds(x_at, 64)], send.at[half], recv.at[group], device),
            remote(g_ref.at[rows], top_ref.at[pl.ds(g_at, 64)], send.at[2 + half], recv.at[2 + group], device),
        )

    def local_moves(half):
        rows = pl.ds(half * 64, 64)
        return (
            pltpu.make_async_copy(x_ref.at[rows], slots_ref.at[pl.ds(x_at, 64)], local.at[0]),
            pltpu.make_async_copy(g_ref.at[rows], top_ref.at[pl.ds(g_at, 64)], local.at[1]),
        )

    for half in (0, 1):

        @pl.when(targets[half] != place.tile)
        def _():
            for copy in moves(half):
                copy.start()

        @pl.when(targets[half] == place.tile)
        def _():
            for copy in local_moves(half):
                copy.start()
            for copy in local_moves(half):
                copy.wait()

    remote(mine, theirs, send.at[12], recv.at[12], (seg, place.cross)).wait_recv()

    def pair(z):
        return all_ref.at[z, place.core]

    def right_copy(step):
        z = (place.z + zs - step) % zs
        return remote(pair(z), pair(z), ring_send.at[0, step], ring_recv.at[0, step], (seg, place.right))

    def left_copy(step):
        z = (place.z + step) % zs
        return remote(pair(z), pair(z), ring_send.at[1, step], ring_recv.at[1, step], (seg, place.left))

    def right_arrival(step):
        z = (place.z + zs - step - 1) % zs
        return remote(pair(z), pair(z), ring_send.at[0, step], ring_recv.at[0, step], (seg, place.right))

    def left_arrival(step):
        z = (place.z + step + 1) % zs
        return remote(pair(z), pair(z), ring_send.at[1, step], ring_recv.at[1, step], (seg, place.left))

    def mate_copy(offset):
        z = (place.z + offset) % zs
        return remote(pair(z), pair(z), mate_send.at[offset], mate_recv.at[offset], (seg, place.mate))

    def mate_arrival(offset):
        z = (place.z + offset) % zs
        block = all_ref.at[z, 1 - place.core]
        return remote(block, block, mate_send.at[offset], mate_recv.at[offset], (seg, place.mate))

    right_steps = zs // 2
    left_steps = zs - 1 - right_steps
    right_copy(0).start()
    left_copy(0).start()
    mate_copy(0).start()
    sides = side_copies(place, slots_ref, T0, send, recv, 4) + side_copies(place, slots_ref, B0, send, recv, 6)
    vertical = Vertical(place, slots_ref, send, recv, 8)
    for step in range(right_steps):
        right_arrival(step).wait_recv()
        if step + 1 < right_steps:
            right_copy(step + 1).start()
        mate_copy(zs - 1 - step).start()
        if step < left_steps:
            left_arrival(step).wait_recv()
            if step + 1 < left_steps:
                left_copy(step + 1).start()
            mate_copy(step + 1).start()
        if step == right_steps // 2 - 1:
            for source, index, own, top in ((place.tile_t, 0, OWN_T, 0), (place.tile_b, 1, OWN_B, 64)):

                @pl.when(source != place.tile)
                def _():
                    remote(
                        x_ref.at[0:64], slots_ref.at[pl.ds(own, 64)], send.at[index], recv.at[index],
                        (seg, place.left),
                    ).wait_recv()
                    remote(
                        g_ref.at[0:64], top_ref.at[pl.ds(top, 64)], send.at[2 + index], recv.at[2 + index],
                        (seg, place.left),
                    ).wait_recv()

            for copy in sides:
                copy.start()
        if step == right_steps - 2:
            for copy in sides:
                copy.wait_recv()
            vertical.start()
    for offset in range(zs):
        mate_arrival(offset).wait_recv()
    vertical.wait_recv()

    over.wait_send()
    for half in (0, 1):

        @pl.when(targets[half] != place.tile)
        def _():
            for copy in moves(half):
                copy.wait_send()

    for copy in sides:
        copy.wait_send()
    vertical.wait_send()
    for step in range(right_steps):
        right_copy(step).wait_send()
    for step in range(left_steps):
        left_copy(step).wait_send()
    for offset in range(zs):
        mate_copy(offset).wait_send()


def gather(pack, x_tokens, g_tokens, tile_count):
    zs = tile_count // 4
    vmem = pl.BlockSpec(memory_space=pltpu.VMEM)
    return pl.pallas_call(
        functools.partial(gather_kernel, tile_count),
        out_shape=(
            jax.ShapeDtypeStruct((zs, 2, 2, 16, WIDE), BF16),
            jax.ShapeDtypeStruct((SLOTS, D), BF16),
            jax.ShapeDtypeStruct((128, D), BF16),
        ),
        in_specs=[vmem] * 3,
        out_specs=(vmem,) * 3,
        scratch_shapes=[
            pltpu.SemaphoreType.DMA((2, zs)),
            pltpu.SemaphoreType.DMA((2, zs)),
            pltpu.SemaphoreType.DMA((zs,)),
            pltpu.SemaphoreType.DMA((zs,)),
            pltpu.SemaphoreType.DMA((13,)),
            pltpu.SemaphoreType.DMA((13,)),
            pltpu.SemaphoreType.DMA((2,)),
        ],
        compiler_params=pltpu.CompilerParams(
            collective_id=0, has_side_effects=True, vmem_limit_bytes=40 * 2**20
        ),
    )(pack, x_tokens, g_tokens)


def dot(left, right):
    return jnp.dot(left, right, preferred_element_type=F32)


def dot_nt(left, right):
    return lax.dot_general(left, right, (((1,), (1,)), ((), ())), preferred_element_type=F32)


def lanes_of(pair, offset=0):
    return pl.ds(pl.multiple_of(offset + pair * 128, 128), 128)


def own_rows(ref, lanes):
    return jnp.concatenate([ref[OWN_T : OWN_T + 64, lanes], ref[OWN_B : OWN_B + 64, lanes]], axis=0)


def put_own(ref, lanes, value):
    ref[OWN_T : OWN_T + 64, lanes] = value[:64]
    ref[OWN_B : OWN_B + 64, lanes] = value[64:]


def first_lanes():
    return lax.broadcasted_iota(jnp.int32, (128, 128), 1) < 64


def split_pair(value):
    low = first_lanes()
    zero = jnp.zeros_like(value)
    return jnp.concatenate([jnp.where(low, value, zero), jnp.where(low, zero, value)], axis=0)


def merge_pair(value):
    return jnp.where(first_lanes(), value[:128], value[128:])


def unpack_weights(all_ref, qkv_ref, out_ref, zs):
    groups = zs * 4 // 16
    rows = lax.broadcasted_iota(jnp.int32, (192, 256), 0)
    cols = lax.broadcasted_iota(jnp.int32, (192, 256), 1)
    yh = rows // 96
    z = (rows % 96) // 24
    core = (rows % 24) // 12
    feature = rows % 12
    shard = z * 4 + core * 2 + yh
    pick = (cols == shard * 16 + feature).astype(F32).astype(BF16)
    half = 96 * groups
    for group in range(groups):

        @pl.loop(0, 9)
        def _(chunk):
            lanes = pl.ds(pl.multiple_of(chunk * 256, 256), 256)
            block = dot(pick, all_ref[group * 256 : (group + 1) * 256, lanes]).astype(BF16)
            qkv_ref[group * 96 : (group + 1) * 96, lanes] = block[:96]
            qkv_ref[half + group * 96 : half + (group + 1) * 96, lanes] = block[96:]

    picks = [
        ((cols == shard * 16 + 12 + feature // 3) & (feature % 3 == part)).astype(F32).astype(BF16)
        for part in range(3)
    ]
    for group in range(groups):

        @pl.loop(0, 3)
        def _(chunk):
            lanes = pl.ds(pl.multiple_of(chunk * 256, 256), 256)
            total = jnp.zeros((192, 256), F32)
            for part in range(3):
                source = pl.ds(pl.multiple_of(part * D + chunk * 256, 256), 256)
                total = total + dot(picks[part], all_ref[group * 256 : (group + 1) * 256, source])
            block = total.astype(BF16)
            out_ref[group * 96 : (group + 1) * 96, lanes] = block[:96]
            out_ref[half + group * 96 : half + (group + 1) * 96, lanes] = block[96:]


def pair_bias(base_ref, side, pair):
    pieces = []
    for head in (0, 1):
        table = base_ref[side, 2 * pair + head]
        for group in (0, 1):
            rows = table[group * 8 : (group + 1) * 8]
            for col in range(8):
                pieces.append(rows if col == 0 else pltpu.roll(rows, 8 * col, axis=1))
    return jnp.concatenate(pieces, axis=0)


def main_kernel(
    tile_count, all_ref, slots_ref, top_ref, base_ref, edge_ref, gain_ref, out_ref,
    qkv_w, out_w, normed, qkv, prob_q, prob_k, ol, gs, ga, po, dqkv, normal, inverse, token, outb,
    lse_acc, rows_acc, send, recv, local,
):
    place = Place(tile_count)
    seg = place.seg
    last_seg = lax.axis_size("segment") - 1
    targets = [place.tile_t, place.tile_b]
    barrier = pltpu.get_barrier_semaphore()
    signal(barrier, (seg, place.left))
    signal(barrier, (seg, place.right))

    @pl.when(place.has_up)
    def _():
        signal(barrier, (seg, place.up))

    @pl.when(place.has_down)
    def _():
        signal(barrier, (seg, place.down))

    @pl.when(seg < last_seg)
    def _():
        signal(barrier, (seg + 1, place.tile))

    count = 2 + one(place.has_up) + one(place.has_down) + one(seg > 0)
    for half in (0, 1):
        source = place.block_of(half)

        @pl.when(source != place.tile)
        def _():
            signal(barrier, (seg, source))

    for target in targets:
        count = count + one(target != place.tile)

    clear_outside(place, ol)
    clear_outside(place, gs)

    unpack_weights(all_ref, qkv_w, out_w, place.zs)

    @pl.loop(0, 5)
    def _(chunk):
        rows = pl.ds(pl.multiple_of(chunk * 128, 128), 128)
        values = slots_ref[rows, :].astype(F32)
        deviation = values - jnp.mean(values, axis=-1, keepdims=True)
        variance = jnp.mean(deviation * deviation, axis=-1, keepdims=True)
        part = deviation * lax.rsqrt(variance + EPSILON)
        normed[rows, :] = (part * gain_ref[...]).astype(BF16)

    own_x = own_rows(slots_ref, slice(0, D)).astype(F32)
    deviation = own_x - jnp.mean(own_x, axis=-1, keepdims=True)
    variance = jnp.mean(deviation * deviation, axis=-1, keepdims=True)
    own_inverse = lax.rsqrt(variance + EPSILON)
    normal[...] = deviation * own_inverse
    inverse[...] = jnp.broadcast_to(own_inverse, (128, 128))

    @pl.loop(0, 9)
    def _(chunk):
        lanes = pl.ds(pl.multiple_of(chunk * 256, 256), 256)
        qkv[:, lanes] = dot(normed[...], qkv_w[:, lanes]).astype(BF16)

    edge = edge_ref[0:1, :]
    lse_acc[...] = jnp.zeros_like(lse_acc)
    head_lane = lax.broadcasted_iota(jnp.int32, (128, 128), 1)

    @pl.loop(0, PAIRS)
    def _(pair):
        query = split_pair(own_rows(qkv, lanes_of(pair)))
        scores = dot_nt(query, qkv[:, lanes_of(pair, D)]) * 0.125 + pair_bias(base_ref, 0, pair) + edge
        top = jnp.max(scores, axis=-1, keepdims=True)
        weight = jnp.exp(scores - top)
        total = jnp.sum(weight, axis=-1, keepdims=True)
        prob = (weight * (1.0 / total)).astype(BF16)
        prob_q[pl.ds(pl.multiple_of(pair * 256, 256), 256), :] = prob
        attn = merge_pair(dot(prob, qkv[:, lanes_of(pair, 2 * D)]))
        put_own(ol, lanes_of(pair), attn.astype(BF16))
        level = top + jnp.log(total)
        lse_acc[...] += jnp.where(head_lane == 2 * pair, level[:128], 0.0) + jnp.where(
            head_lane == 2 * pair + 1, level[128:], 0.0
        )

    level = lse_acc[...]
    high = level.astype(BF16).astype(F32)
    middle = (level - high).astype(BF16).astype(F32)
    low = level - high - middle
    packed = high + pltpu.roll(middle, 16, axis=1) + pltpu.roll(low, 32, axis=1)
    put_own(ol, slice(D, OLW), packed.astype(BF16))

    pl.semaphore_wait(barrier, count)
    ol_sides = side_copies(place, ol, T0, send, recv, 0) + side_copies(place, ol, B0, send, recv, 2)
    ol_vertical = Vertical(place, ol, send, recv, 4)
    for copy in ol_sides:
        copy.start()
    for copy in ol_sides:
        copy.wait_recv()
    ol_vertical.start()
    ol_vertical.wait_recv()

    thirds = lax.broadcasted_iota(jnp.int32, (16, 128), 1)
    head_row = lax.broadcasted_iota(jnp.int32, (16, 128), 0)
    pick = ((thirds < 48) & (thirds % 16 == head_row)).astype(F32).astype(BF16)
    rows_acc[...] = dot_nt(pick, ol[:, D:OLW])

    def pair_rows(pair):
        first = jnp.broadcast_to(rows_acc[pl.ds(2 * pair, 1), :], (128, SLOTS))
        second = jnp.broadcast_to(rows_acc[pl.ds(2 * pair + 1, 1), :], (128, SLOTS))
        return jnp.concatenate([first, second], axis=0)

    @pl.loop(0, PAIRS)
    def _(pair):
        key = split_pair(own_rows(qkv, lanes_of(pair, D)))
        scores = dot_nt(key, qkv[:, lanes_of(pair)]) * 0.125 + pair_bias(base_ref, 1, pair) + edge
        prob_k[pl.ds(pl.multiple_of(pair * 256, 256), 256), :] = jnp.exp(scores - pair_rows(pair)).astype(BF16)

    pass_t = remote(
        outb.at[0:64], gs.at[pl.ds(OWN_T, 64)], send.at[12], recv.at[12], (jnp.maximum(seg - 1, 0), place.tile)
    )
    pass_b = remote(
        outb.at[64:128], gs.at[pl.ds(OWN_B, 64)], send.at[13], recv.at[13], (jnp.maximum(seg - 1, 0), place.tile)
    )
    gs_sides_t = side_copies(place, gs, T0, send, recv, 6)
    gs_sides_b = side_copies(place, gs, B0, send, recv, 8)
    gs_vertical = Vertical(place, gs, send, recv, 10)

    @pl.when(seg == last_seg)
    def _():
        gs[OWN_T : OWN_T + 64, :] = top_ref[0:64, :]
        gs[OWN_B : OWN_B + 64, :] = top_ref[64:128, :]

    pl.when(seg < last_seg)(pass_t.wait_recv)
    for copy in gs_sides_t:
        copy.start()
    pl.when(seg < last_seg)(pass_b.wait_recv)
    for copy in gs_sides_b:
        copy.start()

    own_g = own_rows(gs, slice(0, D))
    for chunk in range(3):
        put_own(
            ga, slice(chunk * 256, (chunk + 1) * 256),
            dot_nt(own_g, out_w[chunk * 256 : (chunk + 1) * 256, :]).astype(BF16),
        )

    for copy in gs_sides_t:
        copy.wait_recv()
    for copy in gs_sides_b:
        copy.wait_recv()
    gs_vertical.start()

    @pl.loop(0, PAIRS)
    def _(pair):
        grad = own_rows(ga, lanes_of(pair))
        product = grad.astype(F32) * own_rows(ol, lanes_of(pair)).astype(F32)
        delta = jnp.sum(split_pair(product), axis=-1, keepdims=True)
        prob_grad = dot_nt(split_pair(grad), qkv[:, lanes_of(pair, 2 * D)])
        prob = prob_q[pl.ds(pl.multiple_of(pair * 256, 256), 256), :].astype(F32)
        score_grad = (prob * (prob_grad - delta)).astype(BF16)
        query_grad = merge_pair(dot(score_grad, qkv[:, lanes_of(pair, D)])) * 0.125
        dqkv[:, lanes_of(pair)] = query_grad.astype(BF16)

    gs_vertical.wait_recv()

    @pl.loop(0, 3)
    def _(chunk):
        rows = pl.ds(pl.multiple_of(chunk * 256, 256), 256)
        ga[:, rows] = dot_nt(gs[...], out_w[rows, :]).astype(BF16)
        po[:, rows] = ga[:, rows] * ol[:, rows]

    wide = lax.broadcasted_iota(jnp.int32, (16, D), 1)
    head_wide = lax.broadcasted_iota(jnp.int32, (16, D), 0)
    pick_wide = (wide // 64 == head_wide).astype(F32).astype(BF16)
    rows_acc[...] = dot_nt(pick_wide, po[...])

    @pl.loop(0, PAIRS)
    def _(pair):
        value = split_pair(own_rows(qkv, lanes_of(pair, 2 * D)))
        prob_grad = dot_nt(value, ga[:, lanes_of(pair)])
        prob = prob_k[pl.ds(pl.multiple_of(pair * 256, 256), 256), :]
        score_grad = (prob.astype(F32) * (prob_grad - pair_rows(pair))).astype(BF16)
        key_grad = merge_pair(dot(score_grad, qkv[:, lanes_of(pair)])) * 0.125
        value_grad = merge_pair(dot(prob, ga[:, lanes_of(pair)]))
        dqkv[:, lanes_of(pair, D)] = key_grad.astype(BF16)
        dqkv[:, lanes_of(pair, 2 * D)] = value_grad.astype(BF16)

    @pl.loop(0, 3)
    def _(chunk):
        rows = pl.ds(pl.multiple_of(chunk * 256, 256), 256)
        token[:, rows] = dot_nt(dqkv[...], qkv_w[rows, :])

    scaled = token[...] * gain_ref[...]
    part = normal[...]
    first_mean = jnp.mean(scaled, axis=-1, keepdims=True)
    second_mean = jnp.mean(scaled * part, axis=-1, keepdims=True)
    branch = inverse[:, 0:1] * (scaled - first_mean - part * second_mean)
    outb[...] = (own_rows(gs, slice(0, D)).astype(F32) + branch).astype(BF16)

    @pl.when(seg > 0)
    def _():
        pass_t.start()
        pass_b.start()

    row_at = pl.multiple_of(place.half * 64, 16)

    def back(group):
        return remote(
            outb.at[pl.ds(group * 64, 64)], out_ref.at[pl.ds(row_at, 64)],
            send.at[14 + group], recv.at[14 + place.half], (seg, targets[group]),
        )

    def back_local(group):
        return pltpu.make_async_copy(outb.at[pl.ds(group * 64, 64)], out_ref.at[pl.ds(row_at, 64)], local.at[group])

    for group in (0, 1):

        @pl.when(targets[group] != place.tile)
        def _():
            back(group).start()

        @pl.when(targets[group] == place.tile)
        def _():
            back_local(group).start()
            back_local(group).wait()

    for half in (0, 1):

        @pl.when(place.block_of(half) != place.tile)
        def _():
            remote(
                outb.at[0:64], out_ref.at[pl.ds(half * 64, 64)], send.at[14 + half], recv.at[14 + half],
                (seg, place.left),
            ).wait_recv()

    for group in (0, 1):

        @pl.when(targets[group] != place.tile)
        def _():
            back(group).wait_send()

    @pl.when(seg > 0)
    def _():
        pass_t.wait_send()
        pass_b.wait_send()

    for copy in ol_sides + gs_sides_t + gs_sides_b:
        copy.wait_send()
    ol_vertical.wait_send()
    gs_vertical.wait_send()


def main(all_weights, slots, top, base, edge, gain, tile_count):
    vmem = pl.BlockSpec(memory_space=pltpu.VMEM)
    return pl.pallas_call(
        functools.partial(main_kernel, tile_count),
        out_shape=jax.ShapeDtypeStruct((128, D), BF16),
        in_specs=[vmem] * 6,
        out_specs=vmem,
        scratch_shapes=[
            pltpu.VMEM((D, WIDE), BF16),
            pltpu.VMEM((D, D), BF16),
            pltpu.VMEM((SLOTS, D), BF16),
            pltpu.VMEM((SLOTS, WIDE), BF16),
            pltpu.VMEM((HEADS * 128, SLOTS), BF16),
            pltpu.VMEM((HEADS * 128, SLOTS), BF16),
            pltpu.VMEM((SLOTS, OLW), BF16),
            pltpu.VMEM((SLOTS, D), BF16),
            pltpu.VMEM((SLOTS, D), BF16),
            pltpu.VMEM((SLOTS, D), BF16),
            pltpu.VMEM((128, WIDE), BF16),
            pltpu.VMEM((128, D), F32),
            pltpu.VMEM((128, 128), F32),
            pltpu.VMEM((128, D), F32),
            pltpu.VMEM((128, D), BF16),
            pltpu.VMEM((128, 128), F32),
            pltpu.VMEM((16, SLOTS), F32),
            pltpu.SemaphoreType.DMA((16,)),
            pltpu.SemaphoreType.DMA((16,)),
            pltpu.SemaphoreType.DMA((2,)),
        ],
        compiler_params=pltpu.CompilerParams(
            collective_id=1, has_side_effects=True, vmem_limit_bytes=56 * 2**20
        ),
    )(all_weights, slots, top, base, edge, gain)


def bias_base(table):
    span = 2 * RAD + 1
    slot = jnp.arange(SLOTS, dtype=jnp.int32)[None, :]
    row = jnp.arange(16, dtype=jnp.int32)[:, None]
    up = 8 * (slot // GROUP - 1) + slot % 8 - row + RAD
    across = (slot % GROUP) // 8 + jnp.zeros_like(row)
    valid = (up >= 0) & (up < span) & (across < span)
    index = jnp.where(valid, up * span + across, -1).reshape(-1)
    onehot = (jnp.arange(span * span, dtype=jnp.int32)[:, None] == index[None, :]).astype(F32)
    both = jnp.stack([table, table[:, ::-1, ::-1]]).reshape(2 * HEADS, span * span)
    base = jnp.dot(both, onehot, precision=lax.Precision.HIGHEST).reshape(2, HEADS, 16, SLOTS)
    return jnp.where(valid[None, None], base, NEG_FILL)


def edge_mask(tile, tile_count):
    zs = tile_count // 4
    z = (tile % (2 * zs)) // 2
    rb = (tile // (2 * zs)) * 2 + tile % 2
    slot = jnp.arange(SLOTS, dtype=jnp.int32)
    group = slot // GROUP
    col = (slot % GROUP) // 8 - RAD
    outside = (
        ((col < 0) & (z == 0)) | ((col > 7) & (z == zs - 1))
        | ((group == 0) & (rb == 0)) | ((group == 3) & (rb == 3))
    )
    return jnp.broadcast_to(jnp.where(outside, NEG_FILL, 0.0)[None], (8, SLOTS)).astype(F32)


def half_tiles(tile):
    return tile.reshape(TH, 2, 8, D).transpose(1, 2, 0, 3).reshape(TH * TW, D)


def body(stored_inputs, output_grads, norm_gain, position_bias, qkv_weight, out_weight):
    tile_count = lax.axis_size("tile")
    tile = lax.axis_index("tile")
    pack = jnp.concatenate([qkv_weight[0], out_weight[0].reshape(-1, WIDE)], axis=0)
    x_tokens = half_tiles(stored_inputs[0, 0, 0])
    g_tokens = half_tiles(output_grads[0, 0])
    gathered, slots, top = gather(pack, x_tokens, g_tokens, tile_count)
    base = bias_base(position_bias[0])
    edge = edge_mask(tile, tile_count)
    out = main(gathered.reshape(-1, WIDE), slots, top, base, edge, norm_gain, tile_count)
    out = out.reshape(2, 8, TH, D).transpose(2, 0, 1, 3).reshape(TH, TW, D)
    return out[None, None, None]


def solution(mesh):
    return jax.shard_map(
        body,
        mesh=mesh,
        in_specs=(
            P("segment", None, "tile", None, None, None),
            P(None, "tile", None, None, None),
            P("segment", None),
            P("segment", None, None, None),
            P("segment", "tile", None),
            P("segment", "tile", None),
        ),
        out_specs=P("segment", None, "tile", None, None, None),
        check_vma=False,
    )
```

time: 1260 us -> 299 us (0.24)
  waiting for transfers between devices: 551 us -> 0 us
  starting transfers between devices: 332 us -> 0 us
  Pallas kernels: 0 us -> 283 us
  local copies, waits for them, and re-layouts: 201 us -> 9.97 us
  other arithmetic: 116 us -> 3.43 us
  matrix products: 32.5 us -> 2.53 us
  between operations: 13.9 us -> 0.08 us
    ppermute x80 -> x0, starting transfers between devices: 332 us -> none  [shifted(): lax.ppermute(value, axis, [(source, source + steps) for source in range(i...]
    pallas_call x0 -> x2, Pallas kernels: none -> 283 us  [the longest x1 204 us: main(): pl.pallas_call(functools.partial(main_kernel, tile_count), out_shape=jax....]
    ppermute x80 -> x0, waiting for transfers between devices: 282 us -> none  [shifted(): lax.ppermute(value, axis, [(source, source + steps) for source in range(i...]
    all_gather x2 -> x0, waiting for transfers between devices: 269 us -> none  [the longest x1 155 us: body(): lax.all_gather(qkv_weight[0], 'tile', axis=0, tiled=True)]
    scatter-add x48 -> x0, local copies, waits for them, and re-layouts: 90.6 us -> none  [return_rim(): summed.at[rim_source(row_step, TH), rim_source(col_step, TW)].add(addend)]
    slice x32 -> x0, local copies, waits for them, and re-layouts: 34 us -> none  [the longest x24 26.2 us: return_rim(): sent = rim_grad[pad_source(row_step, TH), pad_source(col_step, TW)]]
    dot_general x13 -> x1, matrix products: 32.5 us -> 2.53 us  [bias_base(): jnp.dot(both, onehot, precision=lax.Precision.HIGHEST)]
    another operation x32 -> x0, other arithmetic: 29.5 us -> none
  transfers between devices with their start and end apart: 82 -> 0, of which waited for: 21 -> 0; matrix products, arithmetic and copies ran while one was open for 18% -> 0% of each run, Pallas kernels for 0% -> 0%
where the time goes in v1:
time: 299 us
  Pallas kernels  283 us (95%)
  local copies, waits for them, and re-layouts  9.97 us (3%)
  other arithmetic  3.43 us (1%)
    pallas_call x1, Pallas kernels, main(): pl.pallas_call(functools.partial(main_kernel, tile_count), out_shape=jax....  204 us
    pallas_call x1, Pallas kernels, gather(): pl.pallas_call(functools.partial(gather_kernel, tile_count), out_shape=(j...  78.9 us

profile of v1, /device:TPU:1, one launch (start us, length us, event | category | flops | bytes accessed | tf_op | source)
XLA Modules:
  0.0 298.9 jit_solution(11774189722329766011)
XLA Ops:
  0.1 0.6 broadcast_in_dim.39.edge_ref
  0.7 0.8 reshape_squeeze.9
  1.5 0.9 pad_maximum_fusion.pack_ref
  2.4 0.9 copy.22
  3.3 0.1 rev.3
  3.4 0.1 stack.9
  3.5 1.1 reduce
  4.6 0.1 stack.11
  4.7 1.0 copy.11
  5.7 1.0 copy.12
  6.7 2.5 fusion.1
  9.3 1.3 copy_select_fusion.base_ref
  10.6 78.9 %shard_map.64 = (bf16[16,2,2,16,2304]{4,3,2,1,0:T(8,128)(2,1)S(1)}, bf16[640,768]{1,0:T(8,128)(2,1)S(1)}, bf16[128,768]{1,0:T(8,128)(2,1)S(1)}) custom-call(bf16[16,2304]{1,0:T(8,128)(2,1)S(1)} %pad_maximum_fusion.pack_ref, bf16[128,768]{1,0:T(8,128)(2,1)S(1)} %bitcast.28, bf16[128,768]{1,0:T(8,128)(2,1)S(1)} %bitcast.29), custom_call_target="tpu_custom_call" | custom-call | tf_op jit(solution)/shard_map/pallas_call | solution.py:297
  89.5 0.0 copy-start
  89.5 2.1 copy-done
  91.6 0.0 copy-start.1
  91.6 1.0 copy-done.1
  92.6 0.0 copy-start.2
  92.6 0.7 copy-done.2
  93.3 204.0 %shard_map.65 = bf16[128,768]{1,0:T(8,128)(2,1)} custom-call(bf16[1024,2304]{1,0:T(8,128)(2,1)} %bitcast.27, bf16[640,768]{1,0:T(8,128)(2,1)} %copy-done.1, bf16[128,768]{1,0:T(8,128)(2,1)} %copy-done.2, f32[2,12,16,640]{3,2,1,0:T(8,128)} %copy_select_fusion.base_ref, f32[8,640]{1,0:T(8,128)} %broadcast_in_dim.39.edge_ref, f32[1,768]{1,0:T(1,128)} %gain_ref.1), custom_call_target="tpu_custom_call" | custom-call | tf_op jit(solution)/shard_map/pallas_call | solution.py:657
  297.2 1.6 copy.21
  (5 shorter events, 0.1 us)
Async XLA Ops:
  89.5 2.1 copy-start
  91.6 1.0 copy-start.1
  92.6 0.7 copy-start.2

commit v2 on v0

v2 whole, which is shorter than its diff:
```python
import functools
import types

import jax
import jax.numpy as jnp
from jax import lax
from jax.experimental import pallas as pl
from jax.experimental.pallas import tpu as pltpu
from jax.sharding import PartitionSpec as P

D = 768
HEADS = 12
RAD = 6
TH = 8
TW = 16
WIDE = 3 * D
OLW = D + 128
EPSILON = 1e-05
NEG_FILL = -1e30
MESH = pl.DeviceIdType.MESH
BF16 = jnp.bfloat16
F32 = jnp.float32

SLOTS = 640
GROUP = 160
T0, B0 = GROUP, 2 * GROUP
OWN_T, OWN_B = T0 + 48, B0 + 48


class Place:
    def __init__(self, tile_count):
        self.zs = tile_count // 4
        self.cols = self.zs // 2
        self.seg = lax.axis_index("segment")
        self.tile = lax.axis_index("tile")
        self.yh = self.tile // (2 * self.zs)
        self.z = (self.tile % (2 * self.zs)) // 2
        self.core = self.tile % 2
        self.rb = self.yh * 2 + self.core
        self.left = self.at(self.yh, (self.z + self.zs - 1) % self.zs, self.core)
        self.right = self.at(self.yh, (self.z + 1) % self.zs, self.core)
        self.mate = self.at(self.yh, self.z, 1 - self.core)
        self.cross = self.at(1 - self.yh, self.z, self.core)
        self.has_up = self.rb > 0
        self.has_down = self.rb < 3
        up = (self.rb + 3) % 4
        down = (self.rb + 1) % 4
        self.up = self.at(up // 2, self.z, up % 2)
        self.down = self.at(down // 2, self.z, down % 2)
        z_left, z_right = (self.z + self.zs - 1) % self.zs, (self.z + 1) % self.zs
        self.up_left = self.at(up // 2, z_left, up % 2)
        self.up_right = self.at(up // 2, z_right, up % 2)
        self.down_left = self.at(down // 2, z_left, down % 2)
        self.down_right = self.at(down // 2, z_right, down % 2)
        self.row = self.tile // self.cols
        self.col = self.tile % self.cols
        self.half = self.z % 2
        self.tile_t = (2 * self.rb) * self.cols + self.z // 2
        self.tile_b = (2 * self.rb + 1) * self.cols + self.z // 2

    def at(self, yh, z, core):
        return yh * (2 * self.zs) + z * 2 + core

    def block_of(self, half):
        rb = self.row // 2
        return self.at(rb // 2, 2 * self.col + half, rb % 2)


def remote(src, dst, send, recv, device):
    return pltpu.make_async_remote_copy(
        src_ref=src, dst_ref=dst, send_sem=send, recv_sem=recv, device_id=device, device_id_type=MESH
    )


def signal(sem, device):
    pl.semaphore_signal(sem, inc=1, device_id=device, device_id_type=MESH)


def one(flag):
    return jnp.where(flag, 1, 0).astype(jnp.int32)


def clear_outside(place, buf):
    blank = jnp.zeros((GROUP, buf.shape[1]), buf.dtype)

    @pl.when(jnp.logical_not(place.has_up))
    def _():
        buf[0:GROUP, :] = blank

    @pl.when(jnp.logical_not(place.has_down))
    def _():
        buf[3 * GROUP : SLOTS, :] = blank


def dot(left, right):
    return jnp.dot(left, right, preferred_element_type=F32)


def dot_nt(left, right):
    return lax.dot_general(left, right, (((1,), (1,)), ((), ())), preferred_element_type=F32)


def own_rows(ref, lanes):
    return jnp.concatenate([ref[OWN_T : OWN_T + 64, lanes], ref[OWN_B : OWN_B + 64, lanes]], axis=0)


def put_own(ref, lanes, value):
    ref[OWN_T : OWN_T + 64, lanes] = value[:64]
    ref[OWN_B : OWN_B + 64, lanes] = value[64:]


QUADS = 3
WIN = 512


def low_lanes(rows):
    return lax.broadcasted_iota(jnp.int32, (rows, 128), 1) < 64


def split_quad(value):
    low = low_lanes(64)
    zero = jnp.zeros((64, 128), value.dtype)
    rows = []
    for part in (0, 1):
        piece = value[:, part * 128 : (part + 1) * 128]
        for keep in (jnp.where(low, piece, zero), jnp.where(low, zero, piece)):
            rows.append(jnp.concatenate([keep, zero] if part == 0 else [zero, keep], axis=1))
    return jnp.concatenate(rows, axis=0)


def merge_quad(value):
    low = low_lanes(64)
    return jnp.concatenate(
        [
            jnp.where(low, value[0:64, :128], value[64:128, :128]),
            jnp.where(low, value[128:192, 128:], value[192:256, 128:]),
        ],
        axis=1,
    )


def head_sums(value):
    low = low_lanes(64)
    sums = []
    for part in (0, 1):
        piece = value[:, part * 128 : (part + 1) * 128]
        sums.append(jnp.sum(jnp.where(low, piece, 0.0), axis=-1, keepdims=True))
        sums.append(jnp.sum(jnp.where(low, 0.0, piece), axis=-1, keepdims=True))
    return jnp.concatenate(sums, axis=0)


def quad_lanes(quad, offset=0):
    return slice(offset + quad * 256, offset + (quad + 1) * 256)


def window(group):
    return slice(0, WIN) if group == 0 else slice(SLOTS - WIN, SLOTS)


def own(group):
    base = OWN_T if group == 0 else OWN_B
    return slice(base, base + 64)


def quad_bias(base_ref, side, quad, group):
    shift = 0 if group == 0 else GROUP - (SLOTS - WIN)
    pieces = []
    for head in range(4 * quad, 4 * quad + 4):
        rows = base_ref[side, head]
        for col in range(8):
            turn = 8 * col + shift
            pieces.append(rows if turn == 0 else pltpu.roll(rows, turn, axis=1))
    return jnp.concatenate(pieces, axis=0)


def quad_rows(ref, quad, group):
    return jnp.concatenate(
        [jnp.broadcast_to(ref[head : head + 1, window(group)], (64, WIN)) for head in range(4 * quad, 4 * quad + 4)],
        axis=0,
    )


BLOCKS = [(quad, group) for quad in range(QUADS) for group in (0, 1)]


def query_probs(r):
    head_lane = lax.broadcasted_iota(jnp.int32, (64, 128), 1)
    levels = [jnp.zeros((64, 128), F32), jnp.zeros((64, 128), F32)]
    for quad, group in BLOCKS:
        query = split_quad(r.qkv[own(group), quad_lanes(quad)])
        scores = dot_nt(query, r.qkv[window(group), quad_lanes(quad, D)]) * 0.125
        scores = scores + quad_bias(r.base, 0, quad, group) + r.edge[0:1, window(group)]
        top = jnp.max(scores, axis=-1, keepdims=True)
        weight = jnp.exp(scores - top)
        total = jnp.sum(weight, axis=-1, keepdims=True)
        prob = (weight * (1.0 / total)).astype(BF16)
        r.prob_q[quad * 2 + group] = prob
        attn = merge_quad(dot(prob, r.qkv[window(group), quad_lanes(quad, 2 * D)]))
        r.ol[own(group), quad_lanes(quad)] = attn.astype(BF16)
        level = top + jnp.log(total)
        for head in range(4):
            levels[group] = jnp.where(
                head_lane == 4 * quad + head, level[head * 64 : (head + 1) * 64], levels[group]
            )
    for group in (0, 1):
        level = levels[group]
        high = level.astype(BF16).astype(F32)
        middle = (level - high).astype(BF16).astype(F32)
        low = level - high - middle
        packed = high + pltpu.roll(middle, 16, axis=1) + pltpu.roll(low, 32, axis=1)
        r.ol[own(group), D:OLW] = packed.astype(BF16)


def key_probs(r):
    for quad, group in BLOCKS:
        key = split_quad(r.qkv[own(group), quad_lanes(quad, D)])
        scores = dot_nt(key, r.qkv[window(group), quad_lanes(quad)]) * 0.125
        scores = scores + quad_bias(r.base, 1, quad, group) + r.edge[0:1, window(group)]
        r.prob_k[quad * 2 + group] = jnp.exp(scores - quad_rows(r.rows, quad, group)).astype(BF16)


def query_side(r, blocks):
    for quad, group in blocks:
        grad = r.ga[own(group), quad_lanes(quad)]
        delta = head_sums(grad.astype(F32) * r.ol[own(group), quad_lanes(quad)].astype(F32))
        prob_grad = dot_nt(split_quad(grad), r.qkv[window(group), quad_lanes(quad, 2 * D)])
        score_grad = r.prob_q[quad * 2 + group] * (prob_grad - delta).astype(BF16)
        query_grad = merge_quad(dot(score_grad, r.qkv[window(group), quad_lanes(quad, D)])) * 0.125
        r.dqkv[group * 64 : (group + 1) * 64, quad_lanes(quad)] = query_grad.astype(BF16)


def key_side(r):
    for quad, group in BLOCKS:
        value = split_quad(r.qkv[own(group), quad_lanes(quad, 2 * D)])
        prob_grad = dot_nt(value, r.ga[window(group), quad_lanes(quad)])
        prob = r.prob_k[quad * 2 + group]
        score_grad = prob * (prob_grad - quad_rows(r.rows, quad, group)).astype(BF16)
        key_grad = merge_quad(dot(score_grad, r.qkv[window(group), quad_lanes(quad)])) * 0.125
        value_grad = merge_quad(dot(prob, r.ga[window(group), quad_lanes(quad)]))
        rows = slice(group * 64, (group + 1) * 64)
        r.dqkv[rows, quad_lanes(quad, D)] = key_grad.astype(BF16)
        r.dqkv[rows, quad_lanes(quad, 2 * D)] = value_grad.astype(BF16)


def onehot(mask):
    return mask.astype(F32).astype(BF16)


def pack_shard(r, rows):
    at_row = lax.broadcasted_iota(jnp.int32, (16, 12), 0)
    at_col = lax.broadcasted_iota(jnp.int32, (16, 12), 1)
    whole = dot(onehot(at_row == at_col), r.qkv_in[...])
    for part in range(3):
        pick = onehot((at_row == 12 + at_col // 3) & (at_col % 3 == part))
        lanes = slice(part * D, (part + 1) * D)
        r.shards[rows, lanes] = (whole[:, lanes] + dot(pick, r.out_in[...])).astype(BF16)


def unpack_group(r, group, zs):
    rows = lax.broadcasted_iota(jnp.int32, (192, 256), 0)
    cols = lax.broadcasted_iota(jnp.int32, (192, 256), 1)
    shard = ((rows % 96) // 24) * 4 + ((rows % 24) // 12) * 2 + rows // 96
    feature = rows % 12
    source = pl.ds(pl.multiple_of(group * 256, 256), 256)
    low = pl.ds(pl.multiple_of(group * 96, 16), 96)
    high = pl.ds(pl.multiple_of(24 * zs + group * 96, 16), 96)
    block = dot(onehot(cols == shard * 16 + feature), r.shards[source, :]).astype(BF16)
    r.qkv_w[low, :] = block[:96]
    r.qkv_w[high, :] = block[96:]
    total = jnp.zeros((192, D), F32)
    for part in range(3):
        pick = onehot((cols == shard * 16 + 12 + feature // 3) & (feature % 3 == part))
        total = total + dot(pick, r.shards[source, part * D : (part + 1) * D])
    block = total.astype(BF16)
    r.out_w[low, :] = block[:96]
    r.out_w[high, :] = block[96:]


def half_order(rows, cols):
    return onehot(cols == (rows % 8) * TW + (rows // 64) * 8 + (rows % 64) // 8)


def fill_bias(r):
    span = 2 * RAD + 1
    table = r.table[...]
    high = table.astype(BF16)
    rest = table - high.astype(F32)
    middle = rest.astype(BF16)
    low = (rest - middle.astype(F32)).astype(BF16)
    index = lax.broadcasted_iota(jnp.int32, (span * span, WIN), 0)
    slot = lax.broadcasted_iota(jnp.int32, (1, WIN), 1)
    across = (slot % GROUP) // 8
    for row in range(8):
        up = 8 * (slot // GROUP - 1) + slot % 8 - row + RAD
        valid = (up >= 0) & (up < span) & (across < span) & (slot < 3 * GROUP)
        want = up * span + across
        for side in (0, 1):
            pick = onehot(index == (want if side == 0 else span * span - 1 - want))
            value = dot(high, pick) + dot(middle, pick) + dot(low, pick)
            value = jnp.where(valid, value, NEG_FILL)
            for head in range(HEADS):
                r.base[side, head, row : row + 1, :] = value[head : head + 1]


def fill_edge(r, place):
    slot = lax.broadcasted_iota(jnp.int32, (8, SLOTS), 1)
    group = slot // GROUP
    col = (slot % GROUP) // 8 - RAD
    first = jnp.where(place.z == 0, 0, -SLOTS)
    last = jnp.where(place.z == place.zs - 1, 7, SLOTS)
    top = jnp.where(place.has_up, 0, 1)
    bottom = jnp.where(place.has_down, 3, 2)
    outside = (col < first) | (col > last) | (group < top) | (group > bottom)
    r.edge[...] = jnp.where(outside, NEG_FILL, 0.0)


class Ring:
    def __init__(self, place, buf, send, recv, mate_send, mate_recv):
        self.place, self.buf = place, buf
        self.send, self.recv, self.mate_send, self.mate_recv = send, recv, mate_send, mate_recv
        self.half = place.zs // 2

    def rows(self, offset, core, which):
        z = (self.place.z + offset + self.place.zs) % self.place.zs
        yh = self.place.yh if which == 0 else 1 - self.place.yh
        return pl.ds(pl.multiple_of(((z * 2 + core) * 2 + yh) * 16, 16), 16)

    def copy(self, way, step, which, offset):
        part = self.buf.at[self.rows(offset, self.place.core, which)]
        device = self.place.right if way == 0 else self.place.left
        return remote(
            part, part, self.send.at[way, which, step], self.recv.at[way, which, step], (self.place.seg, device)
        )

    def has(self, way, step, which):
        return step < self.half - 1 or (step == self.half - 1 and which == way)

    def leave(self, way, step, which):
        return self.copy(way, step, which, -step if way == 0 else step)

    def arrive(self, way, step, which):
        return self.copy(way, step, which, -step - 1 if way == 0 else step + 1)

    def share(self, offset, which, core=None):
        core = self.place.core if core is None else core
        part = self.buf.at[self.rows(offset, core, which)]
        index = (offset + self.place.zs) % self.place.zs
        return remote(
            part, part, self.mate_send.at[which, index], self.mate_recv.at[which, index],
            (self.place.seg, self.place.mate),
        )

    def begin(self, which):
        self.leave(0, 0, which).start()
        self.leave(1, 0, which).start()
        self.share(0, which).start()

    def turn(self, step):
        for which in (0, 1):
            for way in (0, 1):
                if self.has(way, step, which):
                    self.arrive(way, step, which).wait_recv()
                    if self.has(way, step + 1, which):
                        self.leave(way, step + 1, which).start()
                    self.share(-step - 1 if way == 0 else step + 1, which).start()

    def wait_shared(self, group):
        for member in range(4):
            offset = (group * 4 + member - self.place.z + self.place.zs) % self.place.zs
            for which in (0, 1):
                self.share(offset, which, 1 - self.place.core).wait_recv()

    def wait_send(self):
        for which in (0, 1):
            for way in (0, 1):
                for step in range(self.half):
                    if self.has(way, step, which):
                        self.leave(way, step, which).wait_send()
            for offset in range(self.place.zs):
                self.share(offset, which).wait_send()


class Halo:
    def __init__(self, place, buf, send, recv, at, group):
        base = pl.multiple_of(T0 + group * GROUP, 16)
        over = pl.multiple_of(3 * GROUP * (1 - group), 16)
        self.has = jnp.where(group == 0, one(place.has_up), one(place.has_down)) > 0
        self.gets = jnp.where(group == 0, one(place.has_down), one(place.has_up)) > 0

        def pick(up, down):
            return (place.seg, jnp.where(group == 0, up, down))

        def copy(role, src, rows, dst, device):
            index = at + 5 * group + role
            return remote(
                buf.at[pl.ds(src, rows)], buf.at[pl.ds(dst, rows)], send.at[index], recv.at[index], device
            )

        self.vertical = [
            copy(0, base + 48, 64, over + 48, pick(place.up, place.down)),
            copy(1, base + 48, 48, over + 112, pick(place.up_left, place.down_left)),
            copy(2, base + 64, 48, over, pick(place.up_right, place.down_right)),
        ]
        self.sides = [
            copy(3, base + 48, 48, base + 112, (place.seg, place.left)),
            copy(4, base + 64, 48, base, (place.seg, place.right)),
        ]

    def start(self):
        @pl.when(self.has)
        def _():
            for copy in self.vertical:
                copy.start()

        for copy in self.sides:
            copy.start()

    def wait_sides(self):
        for copy in self.sides:
            copy.wait_recv()

    def wait_vertical(self):
        @pl.when(self.gets)
        def _():
            for copy in self.vertical:
                copy.wait_recv()

    def wait_send(self):
        @pl.when(self.has)
        def _():
            for copy in self.vertical:
                copy.wait_send()

        for copy in self.sides:
            copy.wait_send()


def greet(place, barrier):
    seg = place.seg
    signal(barrier, (seg, place.left))
    signal(barrier, (seg, place.right))

    @pl.when(place.has_up)
    def _():
        for device in (place.up, place.up_left, place.up_right):
            signal(barrier, (seg, device))

    @pl.when(place.has_down)
    def _():
        for device in (place.down, place.down_left, place.down_right):
            signal(barrier, (seg, device))

    return 2 + 3 * one(place.has_up) + 3 * one(place.has_down)


def own_layer_norm(r):
    own_x = own_rows(r.slots, slice(0, D)).astype(F32)
    deviation = own_x - jnp.mean(own_x, axis=-1, keepdims=True)
    variance = jnp.mean(deviation * deviation, axis=-1, keepdims=True)
    own_inverse = lax.rsqrt(variance + EPSILON)
    r.normal[...] = deviation * own_inverse
    r.inverse[...] = jnp.broadcast_to(own_inverse, (128, 128))


def window_layer_norm(r):
    @pl.loop(0, 5)
    def _(chunk):
        rows = pl.ds(pl.multiple_of(chunk * 128, 128), 128)
        values = r.slots[rows, :].astype(F32)
        deviation = values - jnp.mean(values, axis=-1, keepdims=True)
        variance = jnp.mean(deviation * deviation, axis=-1, keepdims=True)
        part = deviation * lax.rsqrt(variance + EPSILON)
        r.normed[rows, :] = (part * r.gain[...]).astype(BF16)


REFS = [
    "x", "g", "gain", "table", "qkv_in", "out_in", "out",
    "shards", "xs", "slots", "top", "qkv_w", "out_w", "qkv_t", "out_t", "normed", "qkv", "prob_q", "prob_k", "ol",
    "gs", "ga", "po", "dqkv", "outb", "got", "normal", "inverse", "token", "rows", "base", "edge",
]


def main_kernel(tile_count, *refs):
    r = types.SimpleNamespace(**dict(zip(REFS, refs)))
    send, recv, local, ring_send, ring_recv, mate_send, mate_recv = refs[len(REFS) :]
    place = Place(tile_count)
    seg, zs = place.seg, place.zs
    last_seg = lax.axis_size("segment") - 1
    tiles = [place.tile_t, place.tile_b]
    blocks = [place.block_of(0), place.block_of(1)]
    barrier = pltpu.get_barrier_semaphore()
    count = greet(place, barrier) + 2 + one(seg > 0)
    signal(barrier, (seg, place.mate))
    signal(barrier, (seg, place.cross))

    @pl.when(seg < last_seg)
    def _():
        signal(barrier, (seg + 1, place.tile))

    for device in tiles + blocks:

        @pl.when(device != place.tile)
        def _():
            signal(barrier, (seg, device))

        count = count + one(device != place.tile)

    ring = Ring(place, r.shards, ring_send, ring_recv, mate_send, mate_recv)
    pack_shard(r, ring.rows(0, place.core, 0))
    new_row = lax.broadcasted_iota(jnp.int32, (128, 128), 0)
    new_col = lax.broadcasted_iota(jnp.int32, (128, 128), 1)
    to_halves = half_order(new_row, new_col)
    r.xs[0:128, :] = dot(to_halves, r.x[...]).astype(BF16)
    for buf in (r.slots, r.ol, r.gs):
        clear_outside(place, buf)
    pl.semaphore_wait(barrier, count)

    mine = r.shards.at[ring.rows(0, place.core, 0)]
    theirs = r.shards.at[ring.rows(0, place.core, 1)]
    over = remote(mine, mine, send.at[44], recv.at[44], (seg, place.cross))
    over.start()
    ring.begin(0)

    tile_group = place.row % 2

    def move(src, half, dst, at):
        row = pl.multiple_of(at, 16)
        return remote(
            r.xs.at[pl.ds(src + half * 64, 64)], dst.at[pl.ds(row, 64)],
            send.at[src // 64 + half], recv.at[src // 64 + tile_group], (seg, blocks[half]),
        )

    def move_local(src, half, dst, at):
        row = pl.multiple_of(at, 16)
        return pltpu.make_async_copy(r.xs.at[pl.ds(src + half * 64, 64)], dst.at[pl.ds(row, 64)], local.at[src // 64 + half])

    def moves_start(src, dst, at):
        for half in (0, 1):

            @pl.when(blocks[half] != place.tile)
            def _():
                move(src, half, dst, at).start()

            @pl.when(blocks[half] == place.tile)
            def _():
                move_local(src, half, dst, at).start()
                move_local(src, half, dst, at).wait()

    def moves_wait_recv(src, dst, rows):
        for group in (0, 1):

            @pl.when(tiles[group] != place.tile)
            def _():
                remote(
                    r.xs.at[0:64], dst.at[rows[group]], send.at[src // 64 + group], recv.at[src // 64 + group],
                    (seg, place.left),
                ).wait_recv()

    def moves_wait_send(src, dst, at):
        for half in (0, 1):

            @pl.when(blocks[half] != place.tile)
            def _():
                move(src, half, dst, at).wait_send()

    x_at = OWN_T + tile_group * GROUP
    g_at = tile_group * 64
    moves_start(0, r.slots, x_at)
    remote(mine, theirs, send.at[44], recv.at[44], (seg, place.cross)).wait_recv()
    ring.begin(1)

    x_halos = [Halo(place, r.slots, send, recv, 4, group) for group in (0, 1)]
    near = jnp.where(place.z % 4 < 2, -1, 1)
    home = place.z // 4
    groups = zs // 4
    for step in range(ring.half):
        ring.turn(step)
        if step == 1:
            fill_edge(r, place)
            fill_bias(r)
        if step == ring.half - 5:
            moves_wait_recv(0, r.slots, [own(0), own(1)])
            for halo in x_halos:
                halo.start()
            own_layer_norm(r)
        if step == ring.half - 4:
            ring.wait_shared(home)
            unpack_group(r, home, zs)
        if step == ring.half - 3:
            ring.wait_shared((home + near + groups) % groups)
            unpack_group(r, (home + near + groups) % groups, zs)
        if step == ring.half - 2:
            for halo in x_halos:
                halo.wait_sides()
                halo.wait_vertical()
            window_layer_norm(r)
            ring.wait_shared((home - near + groups) % groups)
            unpack_group(r, (home - near + groups) % groups, zs)

    @pl.when(seg == last_seg)
    def _():
        r.xs[128:256, :] = dot(to_halves, r.g[...]).astype(BF16)
        moves_start(128, r.top, g_at)

    ring.wait_shared((home + 2) % groups)
    unpack_group(r, (home + 2) % groups, zs)
    r.qkv[...] = dot(r.normed[...], r.qkv_w[...]).astype(BF16)
    query_probs(r)

    ol_halos = [Halo(place, r.ol, send, recv, 14, group) for group in (0, 1)]
    for halo in ol_halos:
        halo.start()
    r.qkv_t[...] = r.qkv_w[...].T
    r.out_t[...] = r.out_w[...].T

    first, second = 1 - place.yh, place.yh

    def passing(group, index):
        rows = pl.multiple_of(group * 64, 16)
        slot = pl.multiple_of(OWN_T + group * GROUP, 16)
        return remote(
            r.outb.at[pl.ds(rows, 64)], r.gs.at[pl.ds(slot, 64)], send.at[index], recv.at[index],
            (jnp.maximum(seg - 1, 0), place.tile),
        )

    passes = [passing(first, 34), passing(second, 35)]
    gs_halos = [Halo(place, r.gs, send, recv, 24, group) for group in (first, second)]

    def as_queries():
        put_own(r.ga, slice(0, D), dot(own_rows(r.gs, slice(0, D)), r.out_t[...]).astype(BF16))
        query_side(r, BLOCKS)
        r.token[...] = dot(r.dqkv[:, 0:D], r.qkv_t[0:D, :])

    @pl.when(seg == last_seg)
    def _():
        moves_wait_recv(128, r.top, [slice(0, 64), slice(64, 128)])
        put_own(r.gs, slice(0, D), r.top[...])
        for halo in gs_halos:
            halo.start()
        as_queries()

    for halo in ol_halos:
        halo.wait_sides()
        halo.wait_vertical()
    thirds = lax.broadcasted_iota(jnp.int32, (16, 128), 1)
    head_row = lax.broadcasted_iota(jnp.int32, (16, 128), 0)
    r.rows[...] = dot_nt(onehot((thirds < 48) & (thirds % 16 == head_row)), r.ol[:, D:OLW])
    key_probs(r)

    @pl.when(seg < last_seg)
    def _():
        for one_pass, halo in zip(passes, gs_halos):
            one_pass.wait_recv()
            halo.start()
        as_queries()

    for halo in gs_halos:
        halo.wait_sides()
    middle = slice(T0, T0 + 2 * GROUP)
    r.ga[middle, :] = dot(r.gs[middle, :], r.out_t[...]).astype(BF16)
    for halo in gs_halos:
        halo.wait_vertical()
    outer = jnp.concatenate([r.gs[0:GROUP, :], r.gs[3 * GROUP : SLOTS, :]], axis=0)
    outer = dot(outer, r.out_t[...]).astype(BF16)
    r.ga[0:GROUP, :] = outer[:GROUP]
    r.ga[3 * GROUP : SLOTS, :] = outer[GROUP:]
    wide = lax.broadcasted_iota(jnp.int32, (16, D), 1)
    head_wide = lax.broadcasted_iota(jnp.int32, (16, D), 0)
    r.po[...] = r.ga[...] * r.ol[:, 0:D]
    r.rows[...] = dot_nt(onehot(wide // 64 == head_wide), r.po[...])
    key_side(r)

    token = r.token[...] + dot(r.dqkv[:, D:WIDE], r.qkv_t[D:WIDE, :])
    scaled = token * r.gain[...]
    part = r.normal[...]
    first_mean = jnp.mean(scaled, axis=-1, keepdims=True)
    second_mean = jnp.mean(scaled * part, axis=-1, keepdims=True)
    branch = r.inverse[:, 0:1] * (scaled - first_mean - part * second_mean)
    r.outb[...] = (own_rows(r.gs, slice(0, D)).astype(F32) + branch).astype(BF16)

    @pl.when(seg > 0)
    def _():
        for one_pass in passes:
            one_pass.start()

    row_at = pl.multiple_of(place.half * 64, 16)

    def back(group):
        return remote(
            r.outb.at[pl.ds(group * 64, 64)], r.got.at[pl.ds(row_at, 64)],
            send.at[36 + group], recv.at[36 + place.half], (seg, tiles[group]),
        )

    def back_local(group):
        return pltpu.make_async_copy(r.outb.at[pl.ds(group * 64, 64)], r.got.at[pl.ds(row_at, 64)], local.at[4 + group])

    for group in (0, 1):

        @pl.when(tiles[group] != place.tile)
        def _():
            back(group).start()

        @pl.when(tiles[group] == place.tile)
        def _():
            back_local(group).start()
            back_local(group).wait()

    ring.wait_send()
    over.wait_send()
    moves_wait_send(0, r.slots, x_at)

    @pl.when(seg == last_seg)
    def _():
        moves_wait_send(128, r.top, g_at)

    for halo in x_halos + ol_halos + gs_halos:
        halo.wait_send()

    for half in (0, 1):

        @pl.when(blocks[half] != place.tile)
        def _():
            remote(
                r.outb.at[0:64], r.got.at[pl.ds(half * 64, 64)], send.at[36 + half], recv.at[36 + half],
                (seg, place.left),
            ).wait_recv()

    r.out[...] = dot(half_order(new_col, new_row), r.got[...]).astype(BF16)

    for group in (0, 1):

        @pl.when(tiles[group] != place.tile)
        def _():
            back(group).wait_send()

    @pl.when(seg > 0)
    def _():
        for one_pass in passes:
            one_pass.wait_send()


def main(x, g, gain, table, qkv_in, out_in, tile_count):
    zs = tile_count // 4
    vmem = pl.BlockSpec(memory_space=pltpu.VMEM)
    bf16 = [
        (zs * 64, WIDE), (256, D), (SLOTS, D), (128, D), (D, WIDE), (D, D), (WIDE, D), (D, D), (SLOTS, D), (SLOTS, WIDE),
        (6, 256, WIN), (6, 256, WIN), (SLOTS, OLW), (SLOTS, D), (SLOTS, D), (SLOTS, D), (128, WIDE), (128, D), (128, D),
    ]
    f32 = [(128, D), (128, 128), (128, D), (16, SLOTS), (2, HEADS, 8, WIN), (8, SLOTS)]
    return pl.pallas_call(
        functools.partial(main_kernel, tile_count),
        out_shape=jax.ShapeDtypeStruct((128, D), BF16),
        in_specs=[vmem] * 6,
        out_specs=vmem,
        scratch_shapes=[pltpu.VMEM(shape, BF16) for shape in bf16]
        + [pltpu.VMEM(shape, F32) for shape in f32]
        + [
            pltpu.SemaphoreType.DMA((45,)),
            pltpu.SemaphoreType.DMA((45,)),
            pltpu.SemaphoreType.DMA((6,)),
            pltpu.SemaphoreType.DMA((2, 2, zs // 2)),
            pltpu.SemaphoreType.DMA((2, 2, zs // 2)),
            pltpu.SemaphoreType.DMA((2, zs)),
            pltpu.SemaphoreType.DMA((2, zs)),
        ],
        compiler_params=pltpu.CompilerParams(
            collective_id=0, has_side_effects=True, vmem_limit_bytes=58 * 2**20
        ),
    )(x, g, gain, table, qkv_in, out_in)


def body(stored_inputs, output_grads, norm_gain, position_bias, qkv_weight, out_weight):
    tokens = TH * TW
    out = main(
        stored_inputs.reshape(tokens, D), output_grads.reshape(tokens, D), norm_gain,
        position_bias.reshape(HEADS, -1), qkv_weight[0], out_weight[0], lax.axis_size("tile"),
    )
    return out.reshape(1, 1, 1, TH, TW, D)


def solution(mesh):
    return jax.shard_map(
        body,
        mesh=mesh,
        in_specs=(
            P("segment", None, "tile", None, None, None),
            P(None, "tile", None, None, None),
            P("segment", None),
            P("segment", None, None, None),
            P("segment", "tile", None),
            P("segment", "tile", None),
        ),
        out_specs=P("segment", None, "tile", None, None, None),
        check_vma=False,
    )
```

time: 1260 us -> 212 us (0.17)
  waiting for transfers between devices: 551 us -> 0 us
  starting transfers between devices: 332 us -> 0 us
  Pallas kernels: 0 us -> 207 us
  local copies, waits for them, and re-layouts: 201 us -> 2.32 us
  other arithmetic: 116 us -> 1.09 us
  matrix products: 32.5 us -> 0 us
  between operations: 13.9 us -> 0.01 us
    ppermute x80 -> x0, starting transfers between devices: 332 us -> none  [shifted(): lax.ppermute(value, axis, [(source, source + steps) for source in range(i...]
    ppermute x80 -> x0, waiting for transfers between devices: 282 us -> none  [shifted(): lax.ppermute(value, axis, [(source, source + steps) for source in range(i...]
    all_gather x2 -> x0, waiting for transfers between devices: 269 us -> none  [the longest x1 155 us: body(): lax.all_gather(qkv_weight[0], 'tile', axis=0, tiled=True)]
    pallas_call x0 -> x1, Pallas kernels: none -> 207 us  [main(): pl.pallas_call(functools.partial(main_kernel, tile_count), out_shape=jax....]
    scatter-add x48 -> x0, local copies, waits for them, and re-layouts: 90.6 us -> none  [return_rim(): summed.at[rim_source(row_step, TH), rim_source(col_step, TW)].add(addend)]
    slice x32 -> x0, local copies, waits for them, and re-layouts: 34 us -> none  [the longest x24 26.2 us: return_rim(): sent = rim_grad[pad_source(row_step, TH), pad_source(col_step, TW)]]
    dot_general x13 -> x0, matrix products: 32.5 us -> none  [the longest x4 7.73 us: dot_trans(): lax.dot_general(left, right, (((1,), (1,)), ((), ())), preferred_element_...]
    another operation x32 -> x0, other arithmetic: 29.5 us -> none
  transfers between devices with their start and end apart: 82 -> 0, of which waited for: 21 -> 0; matrix products, arithmetic and copies ran while one was open for 18% -> 0% of each run, Pallas kernels for 0% -> 0%
where the time goes in v2:
time: 212 us; the launch traced here: 211 us
  Pallas kernels  207 us (98%)
  local copies, waits for them, and re-layouts  2.32 us (1%)
    pallas_call x1, Pallas kernels, main(): pl.pallas_call(functools.partial(main_kernel, tile_count), out_shape=jax....  207 us

profile of v2, /device:TPU:1, one launch (start us, length us, event | category | flops | bytes accessed | tf_op | source)
XLA Modules:
  0.0 210.6 jit_solution(15638620082346108203)
XLA Ops:
  0.0 1.1 reduce
  1.1 0.7 reshape.14.refs_3_
  1.8 207.2 %shard_map.64 = bf16[128,768]{1,0:T(8,128)(2,1)} custom-call(bf16[128,768]{1,0:T(8,128)(2,1)} %bitcast.6, bf16[128,768]{1,0:T(8,128)(2,1)} %bitcast.7, f32[1,768]{1,0:T(1,128)} %refs_2_.1, f32[12,169]{1,0:T(8,128)} %reshape.14.refs_3_, bf16[12,2304]{1,0:T(8,128)(2,1)} %bitcast.8, bf16[12,768]{1,0:T(8,128)(2,1)} %bitcast.9), custom_call_target="tpu_custom_call" | custom-call | tf_op jit(solution)/shard_map/pallas_call | solution.py:750
  209.0 1.6 copy.8

commit v3 on v2

--- a/solution.py
+++ b/solution.py
@@ -52,6 +52,8 @@
         self.up_right = self.at(up // 2, z_right, up % 2)
         self.down_left = self.at(down // 2, z_left, down % 2)
         self.down_right = self.at(down // 2, z_right, down % 2)
+        self.mate_left = self.at(self.yh, z_left, 1 - self.core)
+        self.mate_right = self.at(self.yh, z_right, 1 - self.core)
         self.row = self.tile // self.cols
         self.col = self.tile % self.cols
         self.half = self.z % 2
@@ -381,7 +383,7 @@
 
 
 class Halo:
-    def __init__(self, place, buf, send, recv, at, group):
+    def __init__(self, place, buf, send, recv, at, group, direct=False):
         base = pl.multiple_of(T0 + group * GROUP, 16)
         over = pl.multiple_of(3 * GROUP * (1 - group), 16)
         self.has = jnp.where(group == 0, one(place.has_up), one(place.has_down)) > 0
@@ -396,24 +398,32 @@
                 buf.at[pl.ds(src, rows)], buf.at[pl.ds(dst, rows)], send.at[index], recv.at[index], device
             )
 
-        self.vertical = [
-            copy(0, base + 48, 64, over + 48, pick(place.up, place.down)),
+        self.vertical = [copy(0, base + 48, 64, over + 48, pick(place.up, place.down))]
+        self.corners = [
             copy(1, base + 48, 48, over + 112, pick(place.up_left, place.down_left)),
             copy(2, base + 64, 48, over, pick(place.up_right, place.down_right)),
         ]
+        self.direct = direct
+        self.beyond = self.has & ((group == place.core) if direct else True)
+        self.expects = self.gets & ((group != place.core) if direct else True)
         self.sides = [
             copy(3, base + 48, 48, base + 112, (place.seg, place.left)),
             copy(4, base + 64, 48, base, (place.seg, place.right)),
         ]
 
     def start(self):
+        @pl.when(self.beyond)
+        def _():
+            for copy in self.corners:
+                copy.start()
+
+        for copy in self.sides:
+            copy.start()
+
         @pl.when(self.has)
         def _():
             for copy in self.vertical:
                 copy.start()
-
-        for copy in self.sides:
-            copy.start()
 
     def wait_sides(self):
         for copy in self.sides:
@@ -425,10 +435,20 @@
             for copy in self.vertical:
                 copy.wait_recv()
 
+        @pl.when(self.expects)
+        def _():
+            for copy in self.corners:
+                copy.wait_recv()
+
     def wait_send(self):
         @pl.when(self.has)
         def _():
             for copy in self.vertical:
+                copy.wait_send()
+
+        @pl.when(self.beyond)
+        def _():
+            for copy in self.corners:
                 copy.wait_send()
 
         for copy in self.sides:
@@ -476,7 +496,7 @@
 REFS = [
     "x", "g", "gain", "table", "qkv_in", "out_in", "out",
     "shards", "xs", "slots", "top", "qkv_w", "out_w", "qkv_t", "out_t", "normed", "qkv", "prob_q", "prob_k", "ol",
-    "gs", "ga", "po", "dqkv", "outb", "got", "normal", "inverse", "token", "rows", "base", "edge",
+    "gs", "ga", "po", "dqkv", "outb", "got", "lent", "normal", "inverse", "token", "rows", "base", "edge",
 ]
 
 
@@ -489,13 +509,31 @@
     tiles = [place.tile_t, place.tile_b]
     blocks = [place.block_of(0), place.block_of(1)]
     barrier = pltpu.get_barrier_semaphore()
-    count = greet(place, barrier) + 2 + one(seg > 0)
+    helper = last_seg - 4
+    count = greet(place, barrier) + 2 + 3 * one(seg > 0) + 3 * one(seg == helper) + 5 * one(seg == last_seg)
     signal(barrier, (seg, place.mate))
     signal(barrier, (seg, place.cross))
 
     @pl.when(seg < last_seg)
     def _():
-        signal(barrier, (seg + 1, place.tile))
+        for device in (place.tile, place.mate_left, place.mate_right):
+            signal(barrier, (seg + 1, device))
+
+    @pl.when(seg == last_seg)
+    def _():
+        for device in (place.mate_left, place.mate_right):
+            signal(barrier, (seg, device))
+
+        for device in tiles:
+            signal(barrier, (helper, device))
+
+        signal(barrier, (helper, place.tile))
+
+    @pl.when(seg == helper)
+    def _():
+        signal(barrier, (last_seg, place.tile))
+        for device in blocks:
+            signal(barrier, (last_seg, device))
 
     for device in tiles + blocks:
 
@@ -517,55 +555,74 @@
 
     mine = r.shards.at[ring.rows(0, place.core, 0)]
     theirs = r.shards.at[ring.rows(0, place.core, 1)]
-    over = remote(mine, mine, send.at[44], recv.at[44], (seg, place.cross))
-    over.start()
-    ring.begin(0)
-
     tile_group = place.row % 2
-
-    def move(src, half, dst, at):
-        row = pl.multiple_of(at, 16)
-        return remote(
-            r.xs.at[pl.ds(src + half * 64, 64)], dst.at[pl.ds(row, 64)],
-            send.at[src // 64 + half], recv.at[src // 64 + tile_group], (seg, blocks[half]),
-        )
-
-    def move_local(src, half, dst, at):
-        row = pl.multiple_of(at, 16)
-        return pltpu.make_async_copy(r.xs.at[pl.ds(src + half * 64, 64)], dst.at[pl.ds(row, 64)], local.at[src // 64 + half])
-
-    def moves_start(src, dst, at):
-        for half in (0, 1):
-
-            @pl.when(blocks[half] != place.tile)
-            def _():
-                move(src, half, dst, at).start()
-
-            @pl.when(blocks[half] == place.tile)
-            def _():
-                move_local(src, half, dst, at).start()
-                move_local(src, half, dst, at).wait()
-
-    def moves_wait_recv(src, dst, rows):
-        for group in (0, 1):
-
-            @pl.when(tiles[group] != place.tile)
-            def _():
-                remote(
-                    r.xs.at[0:64], dst.at[rows[group]], send.at[src // 64 + group], recv.at[src // 64 + group],
-                    (seg, place.left),
-                ).wait_recv()
-
-    def moves_wait_send(src, dst, at):
-        for half in (0, 1):
-
-            @pl.when(blocks[half] != place.tile)
-            def _():
-                move(src, half, dst, at).wait_send()
-
     x_at = OWN_T + tile_group * GROUP
     g_at = tile_group * 64
-    moves_start(0, r.slots, x_at)
+
+    def lend(part):
+        rows = pl.ds(part * 128, 128)
+        return remote(r.xs.at[rows], r.lent.at[rows], send.at[45 + part], recv.at[45 + part], (helper, place.tile))
+
+    def forward(part, half):
+        dst, at = ((r.slots, x_at), (r.top, g_at))[part]
+        index = 2 * part + half
+        return remote(
+            r.lent.at[pl.ds(index * 64, 64)], dst.at[pl.ds(pl.multiple_of(at, 16), 64)],
+            send.at[47 + index], recv.at[2 * part + tile_group], (last_seg, blocks[half]),
+        )
+
+    @pl.when(seg == last_seg)
+    def _():
+        lend(0).start()
+        r.xs[128:256, :] = dot(to_halves, r.g[...]).astype(BF16)
+        lend(1).start()
+
+    @pl.when(seg == helper)
+    def _():
+        for part in (0, 1):
+            lend(part).wait_recv()
+            for half in (0, 1):
+                forward(part, half).start()
+        for part in (0, 1):
+            for half in (0, 1):
+                forward(part, half).wait_send()
+
+    cross_send = remote(mine, mine, send.at[44], recv.at[44], (seg, place.cross))
+    cross_send.start()
+    ring.begin(0)
+
+    def move(half):
+        return remote(
+            r.xs.at[pl.ds(half * 64, 64)], r.slots.at[pl.ds(pl.multiple_of(x_at, 16), 64)],
+            send.at[half], recv.at[tile_group], (seg, blocks[half]),
+        )
+
+    def move_local(half):
+        return pltpu.make_async_copy(
+            r.xs.at[pl.ds(half * 64, 64)], r.slots.at[pl.ds(pl.multiple_of(x_at, 16), 64)], local.at[half]
+        )
+
+    for half in (0, 1):
+
+        @pl.when((seg < last_seg) & (blocks[half] != place.tile))
+        def _():
+            move(half).start()
+
+        @pl.when((seg < last_seg) & (blocks[half] == place.tile))
+        def _():
+            move_local(half).start()
+            move_local(half).wait()
+
+    def moves_wait_recv(part, dst, rows):
+        for group in (0, 1):
+
+            @pl.when((seg == last_seg) | (tiles[group] != place.tile))
+            def _():
+                index = 2 * part + group
+                remote(
+                    r.xs.at[0:64], dst.at[rows[group]], send.at[index], recv.at[index], (seg, place.left)
+                ).wait_recv()
+
     remote(mine, theirs, send.at[44], recv.at[44], (seg, place.cross)).wait_recv()
     ring.begin(1)
 
@@ -597,11 +654,6 @@
             ring.wait_shared((home - near + groups) % groups)
             unpack_group(r, (home - near + groups) % groups, zs)
 
-    @pl.when(seg == last_seg)
-    def _():
-        r.xs[128:256, :] = dot(to_halves, r.g[...]).astype(BF16)
-        moves_start(128, r.top, g_at)
-
     ring.wait_shared((home + 2) % groups)
     unpack_group(r, (home + 2) % groups, zs)
     r.qkv[...] = dot(r.normed[...], r.qkv_w[...]).astype(BF16)
@@ -624,7 +676,28 @@
         )
 
     passes = [passing(first, 34), passing(second, 35)]
-    gs_halos = [Halo(place, r.gs, send, recv, 24, group) for group in (first, second)]
+    gs_halos = [Halo(place, r.gs, send, recv, 24, group, True) for group in (first, second)]
+
+    def mate_corners(src, base, device_seg):
+        group = 1 - place.core
+        over = pl.multiple_of(3 * GROUP * (1 - group), 16)
+        return [
+            remote(
+                src.at[pl.ds(pl.multiple_of(base + skip, 16), 48)], r.gs.at[pl.ds(over + land, 48)],
+                send.at[at], recv.at[at], (device_seg, device),
+            )
+            for skip, land, at, device in ((0, 112, 38, place.mate_left), (16, 0, 39, place.mate_right))
+        ]
+
+    below_corners = mate_corners(r.outb, 64 * (1 - place.core), jnp.maximum(seg - 1, 0))
+    top_corners = mate_corners(r.gs, OWN_T + GROUP * (1 - place.core), seg)
+    over = pl.multiple_of(3 * GROUP * (1 - place.core), 16)
+    corner_arrivals = [
+        remote(
+            r.outb.at[0:48], r.gs.at[pl.ds(over + land, 48)], send.at[at], recv.at[at], (seg, place.left)
+        )
+        for land, at in ((112, 38), (0, 39))
+    ]
 
     def as_queries():
         put_own(r.ga, slice(0, D), dot(own_rows(r.gs, slice(0, D)), r.out_t[...]).astype(BF16))
@@ -633,10 +706,12 @@
 
     @pl.when(seg == last_seg)
     def _():
-        moves_wait_recv(128, r.top, [slice(0, 64), slice(64, 128)])
+        moves_wait_recv(1, r.top, [slice(0, 64), slice(64, 128)])
         put_own(r.gs, slice(0, D), r.top[...])
         for halo in gs_halos:
             halo.start()
+        for copy in top_corners:
+            copy.start()
         as_queries()
 
     for halo in ol_halos:
@@ -660,6 +735,8 @@
     r.ga[middle, :] = dot(r.gs[middle, :], r.out_t[...]).astype(BF16)
     for halo in gs_halos:
         halo.wait_vertical()
+    for copy in corner_arrivals:
+        copy.wait_recv()
     outer = jnp.concatenate([r.gs[0:GROUP, :], r.gs[3 * GROUP : SLOTS, :]], axis=0)
     outer = dot(outer, r.out_t[...]).astype(BF16)
     r.ga[0:GROUP, :] = outer[:GROUP]
@@ -682,6 +759,8 @@
     def _():
         for one_pass in passes:
             one_pass.start()
+        for copy in below_corners:
+            copy.start()
 
     row_at = pl.multiple_of(place.half * 64, 16)
 
@@ -706,12 +785,18 @@
             back_local(group).wait()
 
     ring.wait_send()
-    over.wait_send()
-    moves_wait_send(0, r.slots, x_at)
+    cross_send.wait_send()
 
     @pl.when(seg == last_seg)
     def _():
-        moves_wait_send(128, r.top, g_at)
+        lend(0).wait_send()
+        lend(1).wait_send()
+
+    for half in (0, 1):
+
+        @pl.when((seg < last_seg) & (blocks[half] != place.tile))
+        def _():
+            move(half).wait_send()
 
     for halo in x_halos + ol_halos + gs_halos:
         halo.wait_send()
@@ -735,8 +820,13 @@
 
     @pl.when(seg > 0)
     def _():
-        for one_pass in passes:
-            one_pass.wait_send()
+        for copy in passes + below_corners:
+            copy.wait_send()
+
+    @pl.when(seg == last_seg)
+    def _():
+        for copy in top_corners:
+            copy.wait_send()
 
 
 def main(x, g, gain, table, qkv_in, out_in, tile_count):
@@ -745,6 +835,7 @@
     bf16 = [
         (zs * 64, WIDE), (256, D), (SLOTS, D), (128, D), (D, WIDE), (D, D), (WIDE, D), (D, D), (SLOTS, D), (SLOTS, WIDE),
         (6, 256, WIN), (6, 256, WIN), (SLOTS, OLW), (SLOTS, D), (SLOTS, D), (SLOTS, D), (128, WIDE), (128, D), (128, D),
+        (256, D),
     ]
     f32 = [(128, D), (128, 128), (128, D), (16, SLOTS), (2, HEADS, 8, WIN), (8, SLOTS)]
     return pl.pallas_call(
@@ -755,8 +846,8 @@
         scratch_shapes=[pltpu.VMEM(shape, BF16) for shape in bf16]
         + [pltpu.VMEM(shape, F32) for shape in f32]
         + [
-            pltpu.SemaphoreType.DMA((45,)),
-            pltpu.SemaphoreType.DMA((45,)),
+            pltpu.SemaphoreType.DMA((51,)),
+            pltpu.SemaphoreType.DMA((51,)),
             pltpu.SemaphoreType.DMA((6,)),
             pltpu.SemaphoreType.DMA((2, 2, zs // 2)),
             pltpu.SemaphoreType.DMA((2, 2, zs // 2)),

time: 212 us -> 221 us (1.042)
  Pallas kernels: 207 us -> 217 us
    pallas_call x1, Pallas kernels: 207 us -> 217 us  [main(): pl.pallas_call(functools.partial(main_kernel, tile_count), out_shape=jax....]
where the time goes in v3:
time: 221 us
  Pallas kernels  217 us (98%)
  local copies, waits for them, and re-layouts  2.32 us (1%)
    pallas_call x1, Pallas kernels, main(): pl.pallas_call(functools.partial(main_kernel, tile_count), out_shape=jax....  217 us

profile of v3, /device:TPU:1, one launch (start us, length us, event | category | flops | bytes accessed | tf_op | source)
XLA Modules:
  0.0 220.6 jit_solution(13468452406144283592)
XLA Ops:
  0.0 1.1 reduce
  1.1 0.7 reshape.14.refs_3_
  1.8 217.2 %shard_map.64 = bf16[128,768]{1,0:T(8,128)(2,1)} custom-call(bf16[128,768]{1,0:T(8,128)(2,1)} %bitcast.6, bf16[128,768]{1,0:T(8,128)(2,1)} %bitcast.7, f32[1,768]{1,0:T(1,128)} %refs_2_.1, f32[12,169]{1,0:T(8,128)} %reshape.14.refs_3_, bf16[12,2304]{1,0:T(8,128)(2,1)} %bitcast.8, bf16[12,768]{1,0:T(8,128)(2,1)} %bitcast.9), custom_call_target="tpu_custom_call" | custom-call | tf_op jit(solution)/shard_map/pallas_call | solution.py:841
  219.0 1.6 copy.8

commit v4 on v3

--- a/solution.py
+++ b/solution.py
@@ -52,8 +52,6 @@
         self.up_right = self.at(up // 2, z_right, up % 2)
         self.down_left = self.at(down // 2, z_left, down % 2)
         self.down_right = self.at(down // 2, z_right, down % 2)
-        self.mate_left = self.at(self.yh, z_left, 1 - self.core)
-        self.mate_right = self.at(self.yh, z_right, 1 - self.core)
         self.row = self.tile // self.cols
         self.col = self.tile % self.cols
         self.half = self.z % 2
@@ -155,13 +153,20 @@
     return slice(offset + quad * 256, offset + (quad + 1) * 256)
 
 
+def span(start, size, unit):
+    return pl.ds(start if isinstance(start, int) else pl.multiple_of(start, unit), size)
+
+
 def window(group):
-    return slice(0, WIN) if group == 0 else slice(SLOTS - WIN, SLOTS)
+    return span(group * (SLOTS - WIN), WIN, 128)
 
 
 def own(group):
-    base = OWN_T if group == 0 else OWN_B
-    return slice(base, base + 64)
+    return span(OWN_T + group * GROUP, 64, 16)
+
+
+def half(group):
+    return span(group * 64, 64, 16)
 
 
 def quad_bias(base_ref, side, quad, group):
@@ -221,27 +226,55 @@
         r.prob_k[quad * 2 + group] = jnp.exp(scores - quad_rows(r.rows, quad, group)).astype(BF16)
 
 
-def query_side(r, blocks):
-    for quad, group in blocks:
+def query_side(r, group):
+    for quad in range(QUADS):
         grad = r.ga[own(group), quad_lanes(quad)]
         delta = head_sums(grad.astype(F32) * r.ol[own(group), quad_lanes(quad)].astype(F32))
         prob_grad = dot_nt(split_quad(grad), r.qkv[window(group), quad_lanes(quad, 2 * D)])
         score_grad = r.prob_q[quad * 2 + group] * (prob_grad - delta).astype(BF16)
         query_grad = merge_quad(dot(score_grad, r.qkv[window(group), quad_lanes(quad, D)])) * 0.125
-        r.dqkv[group * 64 : (group + 1) * 64, quad_lanes(quad)] = query_grad.astype(BF16)
-
-
-def key_side(r):
-    for quad, group in BLOCKS:
+        r.dqkv[half(group), quad_lanes(quad)] = query_grad.astype(BF16)
+
+
+def key_side(r, group):
+    for quad in range(QUADS):
         value = split_quad(r.qkv[own(group), quad_lanes(quad, 2 * D)])
         prob_grad = dot_nt(value, r.ga[window(group), quad_lanes(quad)])
         prob = r.prob_k[quad * 2 + group]
         score_grad = prob * (prob_grad - quad_rows(r.rows, quad, group)).astype(BF16)
         key_grad = merge_quad(dot(score_grad, r.qkv[window(group), quad_lanes(quad)])) * 0.125
         value_grad = merge_quad(dot(prob, r.ga[window(group), quad_lanes(quad)]))
-        rows = slice(group * 64, (group + 1) * 64)
-        r.dqkv[rows, quad_lanes(quad, D)] = key_grad.astype(BF16)
-        r.dqkv[rows, quad_lanes(quad, 2 * D)] = value_grad.astype(BF16)
+        r.dqkv[half(group), quad_lanes(quad, D)] = key_grad.astype(BF16)
+        r.dqkv[half(group), quad_lanes(quad, 2 * D)] = value_grad.astype(BF16)
+
+
+def attn_grads(r, regions):
+    rows = [span(region * GROUP, GROUP, 16) for region in regions]
+    grads = jnp.concatenate([r.gs[at, :] for at in rows], axis=0)
+    grads = dot(grads, r.out_t[...]).astype(BF16)
+    attn = jnp.concatenate([r.ol[at, 0:D] for at in rows], axis=0)
+    wide = lax.broadcasted_iota(jnp.int32, (16, D), 1)
+    head_wide = lax.broadcasted_iota(jnp.int32, (16, D), 0)
+    deltas = dot_nt(onehot(wide // 64 == head_wide), grads * attn)
+    for index, region in enumerate(regions):
+        part = slice(index * GROUP, (index + 1) * GROUP)
+        r.ga[rows[index], :] = grads[part]
+        r.deltas[region, :, 0:GROUP] = deltas[:, part]
+
+
+def join_deltas(r):
+    r.rows[...] = jnp.concatenate([r.deltas[region, :, 0:GROUP] for region in range(4)], axis=1)
+
+
+def finish(r, group):
+    rows = half(group)
+    token = r.token[rows, :] + dot(r.dqkv[rows, D:WIDE], r.qkv_t[D:WIDE, :])
+    scaled = token * r.gain[...]
+    part = r.normal[rows, :]
+    first_mean = jnp.mean(scaled, axis=-1, keepdims=True)
+    second_mean = jnp.mean(scaled * part, axis=-1, keepdims=True)
+    branch = r.inverse[rows, 0:1] * (scaled - first_mean - part * second_mean)
+    r.outb[rows, :] = (r.gs[own(group), :].astype(F32) + branch).astype(BF16)
 
 
 def onehot(mask):
@@ -383,7 +416,7 @@
 
 
 class Halo:
-    def __init__(self, place, buf, send, recv, at, group, direct=False):
+    def __init__(self, place, buf, send, recv, at, group, relay=False):
         base = pl.multiple_of(T0 + group * GROUP, 16)
         over = pl.multiple_of(3 * GROUP * (1 - group), 16)
         self.has = jnp.where(group == 0, one(place.has_up), one(place.has_down)) > 0
@@ -403,9 +436,8 @@
             copy(1, base + 48, 48, over + 112, pick(place.up_left, place.down_left)),
             copy(2, base + 64, 48, over, pick(place.up_right, place.down_right)),
         ]
-        self.direct = direct
-        self.beyond = self.has & ((group == place.core) if direct else True)
-        self.expects = self.gets & ((group != place.core) if direct else True)
+        self.beyond = self.has & ((group == place.core) if relay else True)
+        self.expects = self.gets & ((group != place.core) if relay else True)
         self.sides = [
             copy(3, base + 48, 48, base + 112, (place.seg, place.left)),
             copy(4, base + 64, 48, base, (place.seg, place.right)),
@@ -496,7 +528,7 @@
 REFS = [
     "x", "g", "gain", "table", "qkv_in", "out_in", "out",
     "shards", "xs", "slots", "top", "qkv_w", "out_w", "qkv_t", "out_t", "normed", "qkv", "prob_q", "prob_k", "ol",
-    "gs", "ga", "po", "dqkv", "outb", "got", "lent", "normal", "inverse", "token", "rows", "base", "edge",
+    "gs", "ga", "dqkv", "outb", "got", "lent", "normal", "inverse", "token", "rows", "deltas", "base", "edge",
 ]
 
 
@@ -510,20 +542,16 @@
     blocks = [place.block_of(0), place.block_of(1)]
     barrier = pltpu.get_barrier_semaphore()
     helper = last_seg - 4
-    count = greet(place, barrier) + 2 + 3 * one(seg > 0) + 3 * one(seg == helper) + 5 * one(seg == last_seg)
+    count = greet(place, barrier) + 2 + one(seg > 0) + 3 * one(seg == helper) + 3 * one(seg == last_seg)
     signal(barrier, (seg, place.mate))
     signal(barrier, (seg, place.cross))
 
     @pl.when(seg < last_seg)
     def _():
-        for device in (place.tile, place.mate_left, place.mate_right):
-            signal(barrier, (seg + 1, device))
+        signal(barrier, (seg + 1, place.tile))
 
     @pl.when(seg == last_seg)
     def _():
-        for device in (place.mate_left, place.mate_right):
-            signal(barrier, (seg, device))
-
         for device in tiles:
             signal(barrier, (helper, device))
 
@@ -535,6 +563,16 @@
         for device in blocks:
             signal(barrier, (last_seg, device))
 
+    @pl.when(seg == 4)
+    def _():
+        signal(barrier, (0, place.tile))
+
+    @pl.when((seg == 0) & (place.row % 2 == 1))
+    def _():
+        for device in blocks:
+            signal(barrier, (4, device))
+
+    count = count + one(seg == 0) + one(seg == 4)
     for device in tiles + blocks:
 
         @pl.when(device != place.tile)
@@ -551,6 +589,8 @@
     r.xs[0:128, :] = dot(to_halves, r.x[...]).astype(BF16)
     for buf in (r.slots, r.ol, r.gs):
         clear_outside(place, buf)
+    r.ga[...] = jnp.zeros_like(r.ga)
+    r.deltas[...] = jnp.zeros_like(r.deltas)
     pl.semaphore_wait(barrier, count)
 
     mine = r.shards.at[ring.rows(0, place.core, 0)]
@@ -563,55 +603,49 @@
         rows = pl.ds(part * 128, 128)
         return remote(r.xs.at[rows], r.lent.at[rows], send.at[45 + part], recv.at[45 + part], (helper, place.tile))
 
-    def forward(part, half):
+    def forward(part, side_half):
         dst, at = ((r.slots, x_at), (r.top, g_at))[part]
-        index = 2 * part + half
+        index = 2 * part + side_half
         return remote(
             r.lent.at[pl.ds(index * 64, 64)], dst.at[pl.ds(pl.multiple_of(at, 16), 64)],
-            send.at[47 + index], recv.at[2 * part + tile_group], (last_seg, blocks[half]),
-        )
-
-    @pl.when(seg == last_seg)
-    def _():
-        lend(0).start()
-        r.xs[128:256, :] = dot(to_halves, r.g[...]).astype(BF16)
-        lend(1).start()
+            send.at[47 + index], recv.at[2 * part + tile_group], (last_seg, blocks[side_half]),
+        )
 
     @pl.when(seg == helper)
     def _():
         for part in (0, 1):
             lend(part).wait_recv()
-            for half in (0, 1):
-                forward(part, half).start()
+            for side_half in (0, 1):
+                forward(part, side_half).start()
         for part in (0, 1):
-            for half in (0, 1):
-                forward(part, half).wait_send()
+            for side_half in (0, 1):
+                forward(part, side_half).wait_send()
 
     cross_send = remote(mine, mine, send.at[44], recv.at[44], (seg, place.cross))
     cross_send.start()
     ring.begin(0)
 
-    def move(half):
+    def move(side_half):
         return remote(
-            r.xs.at[pl.ds(half * 64, 64)], r.slots.at[pl.ds(pl.multiple_of(x_at, 16), 64)],
-            send.at[half], recv.at[tile_group], (seg, blocks[half]),
-        )
-
-    def move_local(half):
+            r.xs.at[pl.ds(side_half * 64, 64)], r.slots.at[pl.ds(pl.multiple_of(x_at, 16), 64)],
+            send.at[side_half], recv.at[tile_group], (seg, blocks[side_half]),
+        )
+
+    def move_local(side_half):
         return pltpu.make_async_copy(
-            r.xs.at[pl.ds(half * 64, 64)], r.slots.at[pl.ds(pl.multiple_of(x_at, 16), 64)], local.at[half]
-        )
-
-    for half in (0, 1):
-
-        @pl.when((seg < last_seg) & (blocks[half] != place.tile))
-        def _():
-            move(half).start()
-
-        @pl.when((seg < last_seg) & (blocks[half] == place.tile))
-        def _():
-            move_local(half).start()
-            move_local(half).wait()
+            r.xs.at[pl.ds(side_half * 64, 64)], r.slots.at[pl.ds(pl.multiple_of(x_at, 16), 64)], local.at[side_half]
+        )
+
+    for side_half in (0, 1):
+
+        @pl.when((seg < last_seg) & (blocks[side_half] != place.tile))
+        def _():
+            move(side_half).start()
+
+        @pl.when((seg < last_seg) & (blocks[side_half] == place.tile))
+        def _():
+            move_local(side_half).start()
+            move_local(side_half).wait()
 
     def moves_wait_recv(part, dst, rows):
         for group in (0, 1):
@@ -626,12 +660,23 @@
     remote(mine, theirs, send.at[44], recv.at[44], (seg, place.cross)).wait_recv()
     ring.begin(1)
 
+    @pl.when(seg == last_seg)
+    def _():
+        lend(0).start()
+        r.xs[128:256, :] = dot(to_halves, r.g[...]).astype(BF16)
+
     x_halos = [Halo(place, r.slots, send, recv, 4, group) for group in (0, 1)]
     near = jnp.where(place.z % 4 < 2, -1, 1)
     home = place.z // 4
     groups = zs // 4
     for step in range(ring.half):
         ring.turn(step)
+        if step == 2:
+
+            @pl.when(seg == last_seg)
+            def _():
+                lend(1).start()
+
         if step == 1:
             fill_edge(r, place)
             fill_bias(r)
@@ -665,7 +710,7 @@
     r.qkv_t[...] = r.qkv_w[...].T
     r.out_t[...] = r.out_w[...].T
 
-    first, second = 1 - place.yh, place.yh
+    first, second = place.core, 1 - place.core
 
     def passing(group, index):
         rows = pl.multiple_of(group * 64, 16)
@@ -678,30 +723,30 @@
     passes = [passing(first, 34), passing(second, 35)]
     gs_halos = [Halo(place, r.gs, send, recv, 24, group, True) for group in (first, second)]
 
-    def mate_corners(src, base, device_seg):
-        group = 1 - place.core
-        over = pl.multiple_of(3 * GROUP * (1 - group), 16)
-        return [
-            remote(
-                src.at[pl.ds(pl.multiple_of(base + skip, 16), 48)], r.gs.at[pl.ds(over + land, 48)],
-                send.at[at], recv.at[at], (device_seg, device),
-            )
-            for skip, land, at, device in ((0, 112, 38, place.mate_left), (16, 0, 39, place.mate_right))
-        ]
-
-    below_corners = mate_corners(r.outb, 64 * (1 - place.core), jnp.maximum(seg - 1, 0))
-    top_corners = mate_corners(r.gs, OWN_T + GROUP * (1 - place.core), seg)
-    over = pl.multiple_of(3 * GROUP * (1 - place.core), 16)
+    relay_group = 1 - place.core
+    side_at = pl.multiple_of(T0 + GROUP * relay_group, 16)
+    over = pl.multiple_of(3 * GROUP * place.core, 16)
+    corners = [
+        remote(
+            r.gs.at[pl.ds(side_at + skip, 48)], r.gs.at[pl.ds(over + skip, 48)],
+            send.at[at], recv.at[at], (seg, place.mate),
+        )
+        for skip, at in ((0, 38), (112, 39))
+    ]
+    over_here = pl.multiple_of(3 * GROUP * (1 - place.core), 16)
     corner_arrivals = [
         remote(
-            r.outb.at[0:48], r.gs.at[pl.ds(over + land, 48)], send.at[at], recv.at[at], (seg, place.left)
-        )
-        for land, at in ((112, 38), (0, 39))
+            r.gs.at[pl.ds(side_at + skip, 48)], r.gs.at[pl.ds(over_here + skip, 48)],
+            send.at[at], recv.at[at], (seg, place.mate),
+        )
+        for skip, at in ((0, 38), (112, 39))
     ]
 
-    def as_queries():
-        put_own(r.ga, slice(0, D), dot(own_rows(r.gs, slice(0, D)), r.out_t[...]).astype(BF16))
-        query_side(r, BLOCKS)
+    def as_queries(group):
+        r.ga[own(group), :] = dot(r.gs[own(group), :], r.out_t[...]).astype(BF16)
+        query_side(r, group)
+
+    def query_tokens():
         r.token[...] = dot(r.dqkv[:, 0:D], r.qkv_t[0:D, :])
 
     @pl.when(seg == last_seg)
@@ -710,9 +755,9 @@
         put_own(r.gs, slice(0, D), r.top[...])
         for halo in gs_halos:
             halo.start()
-        for copy in top_corners:
-            copy.start()
-        as_queries()
+        for group in (0, 1):
+            as_queries(group)
+        query_tokens()
 
     for halo in ol_halos:
         halo.wait_sides()
@@ -724,43 +769,40 @@
 
     @pl.when(seg < last_seg)
     def _():
-        for one_pass, halo in zip(passes, gs_halos):
+        for one_pass, halo, group in zip(passes, gs_halos, (first, second)):
             one_pass.wait_recv()
             halo.start()
-        as_queries()
-
-    for halo in gs_halos:
-        halo.wait_sides()
-    middle = slice(T0, T0 + 2 * GROUP)
-    r.ga[middle, :] = dot(r.gs[middle, :], r.out_t[...]).astype(BF16)
-    for halo in gs_halos:
-        halo.wait_vertical()
+            as_queries(group)
+        query_tokens()
+
+    def send_on(one_pass):
+        pl.when(seg > 0)(one_pass.start)
+
+    gs_halos[0].wait_sides()
+    attn_grads(r, [1 + first])
+    gs_halos[1].wait_sides()
+    for copy in corners:
+        copy.start()
+    gs_halos[1].wait_vertical()
+    attn_grads(r, [1 + second, 3 * first])
+    join_deltas(r)
+    key_side(r, first)
+    finish(r, first)
+    send_on(passes[0])
+
+    gs_halos[0].wait_vertical()
     for copy in corner_arrivals:
         copy.wait_recv()
-    outer = jnp.concatenate([r.gs[0:GROUP, :], r.gs[3 * GROUP : SLOTS, :]], axis=0)
-    outer = dot(outer, r.out_t[...]).astype(BF16)
-    r.ga[0:GROUP, :] = outer[:GROUP]
-    r.ga[3 * GROUP : SLOTS, :] = outer[GROUP:]
-    wide = lax.broadcasted_iota(jnp.int32, (16, D), 1)
-    head_wide = lax.broadcasted_iota(jnp.int32, (16, D), 0)
-    r.po[...] = r.ga[...] * r.ol[:, 0:D]
-    r.rows[...] = dot_nt(onehot(wide // 64 == head_wide), r.po[...])
-    key_side(r)
-
-    token = r.token[...] + dot(r.dqkv[:, D:WIDE], r.qkv_t[D:WIDE, :])
-    scaled = token * r.gain[...]
-    part = r.normal[...]
-    first_mean = jnp.mean(scaled, axis=-1, keepdims=True)
-    second_mean = jnp.mean(scaled * part, axis=-1, keepdims=True)
-    branch = r.inverse[:, 0:1] * (scaled - first_mean - part * second_mean)
-    r.outb[...] = (own_rows(r.gs, slice(0, D)).astype(F32) + branch).astype(BF16)
+    attn_grads(r, [3 * second])
+    join_deltas(r)
+    key_side(r, second)
+    finish(r, second)
+    send_on(passes[1])
 
     @pl.when(seg > 0)
     def _():
         for one_pass in passes:
-            one_pass.start()
-        for copy in below_corners:
-            copy.start()
+            one_pass.wait_send()
 
     row_at = pl.multiple_of(place.half * 64, 16)
 
@@ -773,13 +815,36 @@
     def back_local(group):
         return pltpu.make_async_copy(r.outb.at[pl.ds(group * 64, 64)], r.got.at[pl.ds(row_at, 64)], local.at[4 + group])
 
+    porter = 4
+
+    def hand(chunk):
+        return remote(
+            r.outb.at[pl.ds(64 + chunk * 32, 32)], r.lent.at[pl.ds(chunk * 32, 32)],
+            send.at[51 + chunk], recv.at[51 + chunk], (porter, place.tile),
+        )
+
+    def carry(chunk):
+        row = pl.multiple_of(row_at + chunk * 32, 16)
+        return remote(
+            r.lent.at[pl.ds(chunk * 32, 32)], r.got.at[pl.ds(row, 32)],
+            send.at[53 + chunk], recv.at[40 + 2 * place.half + chunk], (0, tiles[1]),
+        )
+
+    @pl.when(seg == 0)
+    def _():
+        hand(0).start()
+        hand(1).start()
+
+    def straight(group):
+        return True if group == 0 else seg > 0
+
     for group in (0, 1):
 
-        @pl.when(tiles[group] != place.tile)
+        @pl.when((tiles[group] != place.tile) & straight(group))
         def _():
             back(group).start()
 
-        @pl.when(tiles[group] == place.tile)
+        @pl.when((tiles[group] == place.tile) & straight(group))
         def _():
             back_local(group).start()
             back_local(group).wait()
@@ -792,41 +857,59 @@
         lend(0).wait_send()
         lend(1).wait_send()
 
-    for half in (0, 1):
-
-        @pl.when((seg < last_seg) & (blocks[half] != place.tile))
-        def _():
-            move(half).wait_send()
+    for side_half in (0, 1):
+
+        @pl.when((seg < last_seg) & (blocks[side_half] != place.tile))
+        def _():
+            move(side_half).wait_send()
 
     for halo in x_halos + ol_halos + gs_halos:
         halo.wait_send()
-
-    for half in (0, 1):
-
-        @pl.when(blocks[half] != place.tile)
+    for copy in corners:
+        copy.wait_send()
+
+    @pl.when(seg == porter)
+    def _():
+        for chunk in (0, 1):
+            hand(chunk).wait_recv()
+            carry(chunk).start()
+
+    carried = (seg == 0) & (tile_group == 1)
+    for side_half in (0, 1):
+
+        @pl.when((blocks[side_half] != place.tile) & jnp.logical_not(carried))
         def _():
             remote(
-                r.outb.at[0:64], r.got.at[pl.ds(half * 64, 64)], send.at[36 + half], recv.at[36 + half],
+                r.outb.at[0:64], r.got.at[pl.ds(side_half * 64, 64)], send.at[36 + side_half], recv.at[36 + side_half],
                 (seg, place.left),
             ).wait_recv()
 
+        @pl.when(carried)
+        def _():
+            for chunk in (0, 1):
+                index = 40 + 2 * side_half + chunk
+                remote(
+                    r.outb.at[0:32], r.got.at[pl.ds(side_half * 64 + chunk * 32, 32)], send.at[index], recv.at[index],
+                    (seg, place.left),
+                ).wait_recv()
+
     r.out[...] = dot(half_order(new_col, new_row), r.got[...]).astype(BF16)
 
     for group in (0, 1):
 
-        @pl.when(tiles[group] != place.tile)
+        @pl.when((tiles[group] != place.tile) & straight(group))
         def _():
             back(group).wait_send()
 
-    @pl.when(seg > 0)
-    def _():
-        for copy in passes + below_corners:
-            copy.wait_send()
-
-    @pl.when(seg == last_seg)
-    def _():
-        for copy in top_corners:
-            copy.wait_send()
+    @pl.when(seg == 0)
+    def _():
+        hand(0).wait_send()
+        hand(1).wait_send()
+
+    @pl.when(seg == porter)
+    def _():
+        carry(0).wait_send()
+        carry(1).wait_send()
 
 
 def main(x, g, gain, table, qkv_in, out_in, tile_count):
@@ -834,10 +917,10 @@
     vmem = pl.BlockSpec(memory_space=pltpu.VMEM)
     bf16 = [
         (zs * 64, WIDE), (256, D), (SLOTS, D), (128, D), (D, WIDE), (D, D), (WIDE, D), (D, D), (SLOTS, D), (SLOTS, WIDE),
-        (6, 256, WIN), (6, 256, WIN), (SLOTS, OLW), (SLOTS, D), (SLOTS, D), (SLOTS, D), (128, WIDE), (128, D), (128, D),
+        (6, 256, WIN), (6, 256, WIN), (SLOTS, OLW), (SLOTS, D), (SLOTS, D), (128, WIDE), (128, D), (128, D),
         (256, D),
     ]
-    f32 = [(128, D), (128, 128), (128, D), (16, SLOTS), (2, HEADS, 8, WIN), (8, SLOTS)]
+    f32 = [(128, D), (128, 128), (128, D), (16, SLOTS), (4, 16, 256), (2, HEADS, 8, WIN), (8, SLOTS)]
     return pl.pallas_call(
         functools.partial(main_kernel, tile_count),
         out_shape=jax.ShapeDtypeStruct((128, D), BF16),
@@ -846,8 +929,8 @@
         scratch_shapes=[pltpu.VMEM(shape, BF16) for shape in bf16]
         + [pltpu.VMEM(shape, F32) for shape in f32]
         + [
-            pltpu.SemaphoreType.DMA((51,)),
-            pltpu.SemaphoreType.DMA((51,)),
+            pltpu.SemaphoreType.DMA((55,)),
+            pltpu.SemaphoreType.DMA((55,)),
             pltpu.SemaphoreType.DMA((6,)),
             pltpu.SemaphoreType.DMA((2, 2, zs // 2)),
             pltpu.SemaphoreType.DMA((2, 2, zs // 2)),

time: 221 us -> 188 us (0.85); the launches traced: 221 us -> 185 us
  Pallas kernels: 217 us -> 182 us
    pallas_call x1, Pallas kernels: 217 us -> 182 us  [main(): pl.pallas_call(functools.partial(main_kernel, tile_count), out_shape=jax....]
where the time goes in v4:
time: 188 us; the launch traced here: 185 us
  Pallas kernels  182 us (97%)
  local copies, waits for them, and re-layouts  2.32 us (1%)
    pallas_call x1, Pallas kernels, main(): pl.pallas_call(functools.partial(main_kernel, tile_count), out_shape=jax....  182 us

profile of v4, /device:TPU:1, one launch (start us, length us, event | category | flops | bytes accessed | tf_op | source)
XLA Modules:
  0.0 184.9 jit_solution(15688798612645205908)
XLA Ops:
  0.0 1.1 reduce
  1.1 0.7 reshape.14.refs_3_
  1.8 181.5 %shard_map.64 = bf16[128,768]{1,0:T(8,128)(2,1)} custom-call(bf16[128,768]{1,0:T(8,128)(2,1)} %bitcast.6, bf16[128,768]{1,0:T(8,128)(2,1)} %bitcast.7, f32[1,768]{1,0:T(1,128)} %refs_2_.1, f32[12,169]{1,0:T(8,128)} %reshape.14.refs_3_, bf16[12,2304]{1,0:T(8,128)(2,1)} %bitcast.8, bf16[12,768]{1,0:T(8,128)(2,1)} %bitcast.9), custom_call_target="tpu_custom_call" | custom-call | tf_op jit(solution)/shard_map/pallas_call | solution.py:924
  183.3 1.6 copy.8

commit v5 on v4

--- a/solution.py
+++ b/solution.py
@@ -190,10 +190,10 @@
 BLOCKS = [(quad, group) for quad in range(QUADS) for group in (0, 1)]
 
 
-def query_probs(r):
+def query_probs(r, group):
     head_lane = lax.broadcasted_iota(jnp.int32, (64, 128), 1)
-    levels = [jnp.zeros((64, 128), F32), jnp.zeros((64, 128), F32)]
-    for quad, group in BLOCKS:
+    levels = {group: jnp.zeros((64, 128), F32)}
+    for quad in range(QUADS):
         query = split_quad(r.qkv[own(group), quad_lanes(quad)])
         scores = dot_nt(query, r.qkv[window(group), quad_lanes(quad, D)]) * 0.125
         scores = scores + quad_bias(r.base, 0, quad, group) + r.edge[0:1, window(group)]
@@ -209,13 +209,12 @@
             levels[group] = jnp.where(
                 head_lane == 4 * quad + head, level[head * 64 : (head + 1) * 64], levels[group]
             )
-    for group in (0, 1):
-        level = levels[group]
-        high = level.astype(BF16).astype(F32)
-        middle = (level - high).astype(BF16).astype(F32)
-        low = level - high - middle
-        packed = high + pltpu.roll(middle, 16, axis=1) + pltpu.roll(low, 32, axis=1)
-        r.ol[own(group), D:OLW] = packed.astype(BF16)
+    level = levels[group]
+    high = level.astype(BF16).astype(F32)
+    middle = (level - high).astype(BF16).astype(F32)
+    low = level - high - middle
+    packed = high + pltpu.roll(middle, 16, axis=1) + pltpu.roll(low, 32, axis=1)
+    r.ol[own(group), D:OLW] = packed.astype(BF16)
 
 
 def key_probs(r):
@@ -357,18 +356,19 @@
 
     def rows(self, offset, core, which):
         z = (self.place.z + offset + self.place.zs) % self.place.zs
-        yh = self.place.yh if which == 0 else 1 - self.place.yh
+        yh = self.place.yh if which < 2 else 1 - self.place.yh
         return pl.ds(pl.multiple_of(((z * 2 + core) * 2 + yh) * 16, 16), 16)
 
     def copy(self, way, step, which, offset):
-        part = self.buf.at[self.rows(offset, self.place.core, which)]
+        lanes = slice(which % 2 * (WIDE // 2), (which % 2 + 1) * (WIDE // 2))
+        part = self.buf.at[self.rows(offset, self.place.core, which), lanes]
         device = self.place.right if way == 0 else self.place.left
         return remote(
             part, part, self.send.at[way, which, step], self.recv.at[way, which, step], (self.place.seg, device)
         )
 
     def has(self, way, step, which):
-        return step < self.half - 1 or (step == self.half - 1 and which == way)
+        return step < self.half - 1 or (step == self.half - 1 and which // 2 == way)
 
     def leave(self, way, step, which):
         return self.copy(way, step, which, -step if way == 0 else step)
@@ -376,47 +376,50 @@
     def arrive(self, way, step, which):
         return self.copy(way, step, which, -step - 1 if way == 0 else step + 1)
 
-    def share(self, offset, which, core=None):
+    def share(self, offset, shard, core=None):
         core = self.place.core if core is None else core
-        part = self.buf.at[self.rows(offset, core, which)]
+        part = self.buf.at[self.rows(offset, core, 2 * shard)]
         index = (offset + self.place.zs) % self.place.zs
         return remote(
-            part, part, self.mate_send.at[which, index], self.mate_recv.at[which, index],
+            part, part, self.mate_send.at[shard, index], self.mate_recv.at[shard, index],
             (self.place.seg, self.place.mate),
         )
 
-    def begin(self, which):
-        self.leave(0, 0, which).start()
-        self.leave(1, 0, which).start()
-        self.share(0, which).start()
-
-    def turn(self, step):
-        for which in (0, 1):
+    def begin(self, shard):
+        for which in (2 * shard, 2 * shard + 1):
+            self.leave(0, 0, which).start()
+            self.leave(1, 0, which).start()
+        self.share(0, shard).start()
+
+    def turn(self, step, shard):
+        for which in (2 * shard, 2 * shard + 1):
             for way in (0, 1):
                 if self.has(way, step, which):
                     self.arrive(way, step, which).wait_recv()
                     if self.has(way, step + 1, which):
                         self.leave(way, step + 1, which).start()
-                    self.share(-step - 1 if way == 0 else step + 1, which).start()
+                    if which % 2 == 1:
+                        self.share(-step - 1 if way == 0 else step + 1, which // 2).start()
 
     def wait_shared(self, group):
         for member in range(4):
             offset = (group * 4 + member - self.place.z + self.place.zs) % self.place.zs
-            for which in (0, 1):
-                self.share(offset, which, 1 - self.place.core).wait_recv()
+            for shard in (0, 1):
+                self.share(offset, shard, 1 - self.place.core).wait_recv()
 
     def wait_send(self):
-        for which in (0, 1):
+        for which in range(4):
             for way in (0, 1):
                 for step in range(self.half):
                     if self.has(way, step, which):
                         self.leave(way, step, which).wait_send()
+        for shard in (0, 1):
             for offset in range(self.place.zs):
-                self.share(offset, which).wait_send()
+                self.share(offset, shard).wait_send()
 
 
 class Halo:
-    def __init__(self, place, buf, send, recv, at, group, relay=False):
+    def __init__(self, place, buf, send, recv, at, group, relay=False, more=0):
         base = pl.multiple_of(T0 + group * GROUP, 16)
         over = pl.multiple_of(3 * GROUP * (1 - group), 16)
         self.has = jnp.where(group == 0, one(place.has_up), one(place.has_down)) > 0
@@ -438,27 +441,42 @@
         ]
         self.beyond = self.has & ((group == place.core) if relay else True)
         self.expects = self.gets & ((group != place.core) if relay else True)
-        self.sides = [
-            copy(3, base + 48, 48, base + 112, (place.seg, place.left)),
-            copy(4, base + 64, 48, base, (place.seg, place.right)),
-        ]
-
-    def start(self):
+        left, right = (place.seg, place.left), (place.seg, place.right)
+        self.rest = []
+        if more:
+            self.sides = [copy(3, base + 48, 32, base + 112, left), copy(4, base + 64, 16, base, right)]
+            self.rest = [
+                remote(buf.at[pl.ds(base + src, rows)], buf.at[pl.ds(base + dst, rows)], send.at[index], recv.at[index], device)
+                for src, rows, dst, index, device in ((80, 16, 144, more, left), (80, 32, 16, more + 1, right))
+            ]
+        else:
+            self.sides = [copy(3, base + 48, 48, base + 112, left), copy(4, base + 64, 48, base, right)]
+
+    def start_sides(self):
+        for copy in self.sides:
+            copy.start()
+
+    def start_vertical(self):
+        @pl.when(self.has)
+        def _():
+            for copy in self.vertical:
+                copy.start()
+
         @pl.when(self.beyond)
         def _():
             for copy in self.corners:
                 copy.start()
 
-        for copy in self.sides:
+    def start(self, sides=True):
+        if not self.rest:
+            self.start_vertical()
+        for copy in (self.sides if sides else []) + self.rest:
             copy.start()
-
-        @pl.when(self.has)
-        def _():
-            for copy in self.vertical:
-                copy.start()
+        if self.rest:
+            self.start_vertical()
 
     def wait_sides(self):
-        for copy in self.sides:
+        for copy in self.sides + self.rest:
             copy.wait_recv()
 
     def wait_vertical(self):
@@ -483,7 +501,7 @@
             for copy in self.corners:
                 copy.wait_send()
 
-        for copy in self.sides:
+        for copy in self.sides + self.rest:
             copy.wait_send()
 
 
@@ -594,7 +612,7 @@
     pl.semaphore_wait(barrier, count)
 
     mine = r.shards.at[ring.rows(0, place.core, 0)]
-    theirs = r.shards.at[ring.rows(0, place.core, 1)]
+    theirs = r.shards.at[ring.rows(0, place.core, 2)]
     tile_group = place.row % 2
     x_at = OWN_T + tile_group * GROUP
     g_at = tile_group * 64
@@ -657,6 +675,9 @@
                     r.xs.at[0:64], dst.at[rows[group]], send.at[index], recv.at[index], (seg, place.left)
                 ).wait_recv()
 
+    ring.turn(0, 0)
+    fill_edge(r, place)
+    fill_bias(r)
     remote(mine, theirs, send.at[44], recv.at[44], (seg, place.cross)).wait_recv()
     ring.begin(1)
 
@@ -670,22 +691,20 @@
     home = place.z // 4
     groups = zs // 4
     for step in range(ring.half):
-        ring.turn(step)
+        ring.turn(step, 1)
+        if step + 1 < ring.half:
+            ring.turn(step + 1, 0)
         if step == 2:
 
             @pl.when(seg == last_seg)
             def _():
                 lend(1).start()
 
-        if step == 1:
-            fill_edge(r, place)
-            fill_bias(r)
-        if step == ring.half - 5:
+        if step == ring.half - 4:
             moves_wait_recv(0, r.slots, [own(0), own(1)])
             for halo in x_halos:
                 halo.start()
             own_layer_norm(r)
-        if step == ring.half - 4:
             ring.wait_shared(home)
             unpack_group(r, home, zs)
         if step == ring.half - 3:
@@ -702,26 +721,28 @@
     ring.wait_shared((home + 2) % groups)
     unpack_group(r, (home + 2) % groups, zs)
     r.qkv[...] = dot(r.normed[...], r.qkv_w[...]).astype(BF16)
-    query_probs(r)
-
     ol_halos = [Halo(place, r.ol, send, recv, 14, group) for group in (0, 1)]
-    for halo in ol_halos:
-        halo.start()
+    for group in (0, 1):
+        query_probs(r, group)
+        ol_halos[group].start()
     r.qkv_t[...] = r.qkv_w[...].T
     r.out_t[...] = r.out_w[...].T
 
     first, second = place.core, 1 - place.core
 
-    def passing(group, index):
-        rows = pl.multiple_of(group * 64, 16)
-        slot = pl.multiple_of(OWN_T + group * GROUP, 16)
+    def passing(group, skip, size, index):
+        row = pl.multiple_of(group * 64 + skip, 16)
+        slot = pl.multiple_of(OWN_T + group * GROUP + skip, 16)
         return remote(
-            r.outb.at[pl.ds(rows, 64)], r.gs.at[pl.ds(slot, 64)], send.at[index], recv.at[index],
+            r.outb.at[pl.ds(row, size)], r.gs.at[pl.ds(slot, size)], send.at[index], recv.at[index],
             (jnp.maximum(seg - 1, 0), place.tile),
         )
 
-    passes = [passing(first, 34), passing(second, 35)]
-    gs_halos = [Halo(place, r.gs, send, recv, 24, group, True) for group in (first, second)]
+    passes = [passing(first, 0, 64, 34), passing(second, 0, 32, 35), passing(second, 32, 32, 55)]
+    gs_halos = [
+        Halo(place, r.gs, send, recv, 24, first, True),
+        Halo(place, r.gs, send, recv, 24, second, True, 56),
+    ]
 
     relay_group = 1 - place.core
     side_at = pl.multiple_of(T0 + GROUP * relay_group, 16)
@@ -769,26 +790,81 @@
 
     @pl.when(seg < last_seg)
     def _():
-        for one_pass, halo, group in zip(passes, gs_halos, (first, second)):
-            one_pass.wait_recv()
-            halo.start()
-            as_queries(group)
+        passes[0].wait_recv()
+        gs_halos[0].start()
+        as_queries(first)
+        passes[1].wait_recv()
+        gs_halos[1].start_sides()
+        passes[2].wait_recv()
+        gs_halos[1].start(sides=False)
+        as_queries(second)
         query_tokens()
 
-    def send_on(one_pass):
-        pl.when(seg > 0)(one_pass.start)
+    row_at = pl.multiple_of(place.half * 64, 16)
+
+    def back(group):
+        return remote(
+            r.outb.at[pl.ds(group * 64, 64)], r.got.at[pl.ds(row_at, 64)],
+            send.at[36 + group], recv.at[36 + place.half], (seg, tiles[group]),
+        )
+
+    def back_local(group):
+        return pltpu.make_async_copy(r.outb.at[pl.ds(group * 64, 64)], r.got.at[pl.ds(row_at, 64)], local.at[4 + group])
+
+    porter = 4
+
+    def hand(chunk):
+        return remote(
+            r.outb.at[pl.ds(64 + chunk * 32, 32)], r.lent.at[pl.ds(chunk * 32, 32)],
+            send.at[51 + chunk], recv.at[51 + chunk], (porter, place.tile),
+        )
+
+    def carry(chunk):
+        row = pl.multiple_of(row_at + chunk * 32, 16)
+        return remote(
+            r.lent.at[pl.ds(chunk * 32, 32)], r.got.at[pl.ds(row, 32)],
+            send.at[53 + chunk], recv.at[40 + 2 * place.half + chunk], (0, tiles[1]),
+        )
+
+    def straight(group):
+        return True if group == 0 else seg > 0
+
+    def go_back(group, when):
+        @pl.when((tiles[group] != place.tile) & when)
+        def _():
+            back(group).start()
+
+        @pl.when((tiles[group] == place.tile) & when)
+        def _():
+            back_local(group).start()
+            back_local(group).wait()
+
+    def go_home(upper):
+        go_back(0, (seg == 0) & upper)
+
+        @pl.when((seg == 0) & jnp.logical_not(upper))
+        def _():
+            hand(0).start()
+            hand(1).start()
+
+    def send_on(copies):
+        @pl.when(seg > 0)
+        def _():
+            for copy in copies:
+                copy.start()
 
     gs_halos[0].wait_sides()
-    attn_grads(r, [1 + first])
+    gs_halos[1].wait_vertical()
+    attn_grads(r, [1 + first, 3 * first])
     gs_halos[1].wait_sides()
     for copy in corners:
         copy.start()
-    gs_halos[1].wait_vertical()
-    attn_grads(r, [1 + second, 3 * first])
+    attn_grads(r, [1 + second])
     join_deltas(r)
     key_side(r, first)
     finish(r, first)
-    send_on(passes[0])
+    send_on(passes[:1])
+    go_home(first == 0)
 
     gs_halos[0].wait_vertical()
     for copy in corner_arrivals:
@@ -797,57 +873,16 @@
     join_deltas(r)
     key_side(r, second)
     finish(r, second)
-    send_on(passes[1])
+    send_on(passes[1:])
+    go_home(second == 0)
 
     @pl.when(seg > 0)
     def _():
         for one_pass in passes:
             one_pass.wait_send()
 
-    row_at = pl.multiple_of(place.half * 64, 16)
-
-    def back(group):
-        return remote(
-            r.outb.at[pl.ds(group * 64, 64)], r.got.at[pl.ds(row_at, 64)],
-            send.at[36 + group], recv.at[36 + place.half], (seg, tiles[group]),
-        )
-
-    def back_local(group):
-        return pltpu.make_async_copy(r.outb.at[pl.ds(group * 64, 64)], r.got.at[pl.ds(row_at, 64)], local.at[4 + group])
-
-    porter = 4
-
-    def hand(chunk):
-        return remote(
-            r.outb.at[pl.ds(64 + chunk * 32, 32)], r.lent.at[pl.ds(chunk * 32, 32)],
-            send.at[51 + chunk], recv.at[51 + chunk], (porter, place.tile),
-        )
-
-    def carry(chunk):
-        row = pl.multiple_of(row_at + chunk * 32, 16)
-        return remote(
-            r.lent.at[pl.ds(chunk * 32, 32)], r.got.at[pl.ds(row, 32)],
-            send.at[53 + chunk], recv.at[40 + 2 * place.half + chunk], (0, tiles[1]),
-        )
-
-    @pl.when(seg == 0)
-    def _():
-        hand(0).start()
-        hand(1).start()
-
-    def straight(group):
-        return True if group == 0 else seg > 0
-
     for group in (0, 1):
-
-        @pl.when((tiles[group] != place.tile) & straight(group))
-        def _():
-            back(group).start()
-
-        @pl.when((tiles[group] == place.tile) & straight(group))
-        def _():
-            back_local(group).start()
-            back_local(group).wait()
+        go_back(group, seg > 0)
 
     ring.wait_send()
     cross_send.wait_send()
@@ -929,11 +964,11 @@
         scratch_shapes=[pltpu.VMEM(shape, BF16) for shape in bf16]
         + [pltpu.VMEM(shape, F32) for shape in f32]
         + [
-            pltpu.SemaphoreType.DMA((55,)),
-            pltpu.SemaphoreType.DMA((55,)),
+            pltpu.SemaphoreType.DMA((58,)),
+            pltpu.SemaphoreType.DMA((58,)),
             pltpu.SemaphoreType.DMA((6,)),
-            pltpu.SemaphoreType.DMA((2, 2, zs // 2)),
-            pltpu.SemaphoreType.DMA((2, 2, zs // 2)),
+            pltpu.SemaphoreType.DMA((2, 4, zs // 2)),
+            pltpu.SemaphoreType.DMA((2, 4, zs // 2)),
             pltpu.SemaphoreType.DMA((2, zs)),
             pltpu.SemaphoreType.DMA((2, zs)),
         ],

time: 188 us -> 184 us (0.979); the launches traced: 185 us -> 184 us
  Pallas kernels: 182 us -> 180 us
where the time goes in v5:
time: 184 us
  Pallas kernels  180 us (98%)
  local copies, waits for them, and re-layouts  2.32 us (1%)
    pallas_call x1, Pallas kernels, main(): pl.pallas_call(functools.partial(main_kernel, tile_count), out_shape=jax....  180 us

profile of v5, /device:TPU:1, one launch (start us, length us, event | category | flops | bytes accessed | tf_op | source)
XLA Modules:
  0.0 183.8 jit_solution(6037108413331551554)
XLA Ops:
  0.0 1.1 reduce
  1.1 0.7 reshape.14.refs_3_
  1.8 180.4 %shard_map.64 = bf16[128,768]{1,0:T(8,128)(2,1)} custom-call(bf16[128,768]{1,0:T(8,128)(2,1)} %bitcast.6, bf16[128,768]{1,0:T(8,128)(2,1)} %bitcast.7, f32[1,768]{1,0:T(1,128)} %refs_2_.1, f32[12,169]{1,0:T(8,128)} %reshape.14.refs_3_, bf16[12,2304]{1,0:T(8,128)(2,1)} %bitcast.8, bf16[12,768]{1,0:T(8,128)(2,1)} %bitcast.9), custom_call_target="tpu_custom_call" | custom-call | tf_op jit(solution)/shard_map/pallas_call | solution.py:959
  182.2 1.6 copy.8

commit v6 on v5

--- a/solution.py
+++ b/solution.py
@@ -585,7 +585,7 @@
     def _():
         signal(barrier, (0, place.tile))
 
-    @pl.when((seg == 0) & (place.row % 2 == 1))
+    @pl.when((seg == 0) & (place.row % 2 == (place.row // 2) % 2))
     def _():
         for device in blocks:
             signal(barrier, (4, device))
@@ -815,7 +815,7 @@
 
     def hand(chunk):
         return remote(
-            r.outb.at[pl.ds(64 + chunk * 32, 32)], r.lent.at[pl.ds(chunk * 32, 32)],
+            r.outb.at[pl.ds(pl.multiple_of(first * 64 + chunk * 32, 16), 32)], r.lent.at[pl.ds(chunk * 32, 32)],
             send.at[51 + chunk], recv.at[51 + chunk], (porter, place.tile),
         )
 
@@ -823,11 +823,11 @@
         row = pl.multiple_of(row_at + chunk * 32, 16)
         return remote(
             r.lent.at[pl.ds(chunk * 32, 32)], r.got.at[pl.ds(row, 32)],
-            send.at[53 + chunk], recv.at[40 + 2 * place.half + chunk], (0, tiles[1]),
+            send.at[53 + chunk], recv.at[40 + 2 * place.half + chunk], (0, jnp.where(first == 0, tiles[0], tiles[1])),
         )
 
     def straight(group):
-        return True if group == 0 else seg > 0
+        return (seg > 0) | (second == group)
 
     def go_back(group, when):
         @pl.when((tiles[group] != place.tile) & when)
@@ -839,10 +839,8 @@
             back_local(group).start()
             back_local(group).wait()
 
-    def go_home(upper):
-        go_back(0, (seg == 0) & upper)
-
-        @pl.when((seg == 0) & jnp.logical_not(upper))
+    def hand_over():
+        @pl.when(seg == 0)
         def _():
             hand(0).start()
             hand(1).start()
@@ -864,7 +862,7 @@
     key_side(r, first)
     finish(r, first)
     send_on(passes[:1])
-    go_home(first == 0)
+    hand_over()
 
     gs_halos[0].wait_vertical()
     for copy in corner_arrivals:
@@ -874,7 +872,8 @@
     key_side(r, second)
     finish(r, second)
     send_on(passes[1:])
-    go_home(second == 0)
+    for group in (0, 1):
+        go_back(group, (seg == 0) & (second == group))
 
     @pl.when(seg > 0)
     def _():
@@ -909,7 +908,7 @@
             hand(chunk).wait_recv()
             carry(chunk).start()
 
-    carried = (seg == 0) & (tile_group == 1)
+    carried = (seg == 0) & (tile_group == (place.row // 2) % 2)
     for side_half in (0, 1):
 
         @pl.when((blocks[side_half] != place.tile) & jnp.logical_not(carried))

time: 184 us -> 190 us (1.033)
  Pallas kernels: 180 us -> 186 us
    pallas_call x1, Pallas kernels: 180 us -> 186 us  [main(): pl.pallas_call(functools.partial(main_kernel, tile_count), out_shape=jax....]
where the time goes in v6:
time: 190 us; the launch traced here: 189 us
  Pallas kernels  186 us (98%)
  local copies, waits for them, and re-layouts  2.32 us (1%)
    pallas_call x1, Pallas kernels, main(): pl.pallas_call(functools.partial(main_kernel, tile_count), out_shape=jax....  186 us

profile of v6, /device:TPU:1, one launch (start us, length us, event | category | flops | bytes accessed | tf_op | source)
XLA Modules:
  0.0 189.4 jit_solution(17026010158957079549)
XLA Ops:
  0.0 1.1 reduce
  1.1 0.7 reshape.14.refs_3_
  1.8 185.9 %shard_map.64 = bf16[128,768]{1,0:T(8,128)(2,1)} custom-call(bf16[128,768]{1,0:T(8,128)(2,1)} %bitcast.6, bf16[128,768]{1,0:T(8,128)(2,1)} %bitcast.7, f32[1,768]{1,0:T(1,128)} %refs_2_.1, f32[12,169]{1,0:T(8,128)} %reshape.14.refs_3_, bf16[12,2304]{1,0:T(8,128)(2,1)} %bitcast.8, bf16[12,768]{1,0:T(8,128)(2,1)} %bitcast.9), custom_call_target="tpu_custom_call" | custom-call | tf_op jit(solution)/shard_map/pallas_call | solution.py:958
  187.7 1.6 copy.8
